TPU v7x, 512 devices: a whole 4x4x16 slice. The times are simulated.
512 devices in a mesh: ctx: 32 (over y, x, core), head: 16 (over z).
Axes of the slice: x: 4, y: 4, z: 16, core: 2. Of those that a mesh axis runs over, the one named last changes fastest.
Arguments:
- queries: bfloat16 [8192, 4096], P('ctx', 'head'), may hold values from -50 to 50
- keys: bfloat16 [8192, 4096], P('ctx', 'head'), may hold values from -9 to 9
- values: bfloat16 [8192, 4096], P('ctx', 'head'), may hold values from -9 to 9
- near_blocks: int32 [64, 4], P('ctx'), may hold values from 0 to 63, as said below
- near_count: int32 [64], P('ctx'), may hold values from 1 to 4
- head_scale: float32 [32], P('head'), may hold values from 0.2 to 4.2
- gain: float32 [4096], P('head'), may hold values from 0.5 to 1.5
- cotangent: bfloat16 [8192, 4096], P('ctx', 'head'), may hold values from -6 to 6
Outputs:
- mixed: bfloat16 [8192, 4096], P('ctx', 'head')
- grad_queries: bfloat16 [8192, 4096], P('ctx', 'head')
- grad_keys: bfloat16 [8192, 4096], P('ctx', 'head')
- grad_values: bfloat16 [8192, 4096], P('ctx', 'head')
Inputs may be any that keep to these rules, and one draw needn't show every extreme that they name: near_blocks[b, 0] = b; entries 1 to near_count[b] - 1 are distinct blocks other than b within 2 blocks of b; the later entries equal b.
All inputs are finite; a program needn't handle non-finite values.
Results may differ from a plain program's by a relative error of at most 0.022.
Values may be sent and summed in bfloat16 or wider, within the bound.
A program may use at most 64 MiB of HBM per device.

v0:
```python
import math

import jax
import jax.numpy as jnp
from jax import lax
from jax.sharding import PartitionSpec as P

HEADS = 32
HEAD_SIZE = 128
BLOCK_TOKENS = 128
NEAR_SLOTS = 4
RB = 2
LEV = 5


LOG_TWO = 0.6931471805599453
NEG_BIG = -1e30
NORM_EPS = 1e-05


def padded_2(cells, sides, width):
    for axis, dim in sides:
        count = lax.axis_size(axis)
        ends = count - 1
        head = lax.slice_in_dim(cells, 0, width, axis=dim)
        tail = lax.slice_in_dim(cells, cells.shape[dim] - width, cells.shape[dim], axis=dim)
        cells = jnp.concatenate(
            [
                lax.ppermute(tail, axis, [(i, (i + 1) % count) for i in range(ends)]),
                cells,
                lax.ppermute(head, axis, [((i + 1) % count, i) for i in range(ends)]),
            ],
            axis=dim,
        )
    return cells


def passed_along(value, axis, by):
    size = lax.axis_size(axis)
    pairs = [(i, i + by) for i in range(size) if 0 <= i + by < size]
    return lax.ppermute(value, axis, pairs)


def shortened(value):

    def short(part):
        return part.astype(jnp.bfloat16) if part.dtype == jnp.float32 else part

    return jax.tree.map(short, value)


def from_partner(value, axis, apart):
    mask = 2**apart
    pairs = [(source, source ^ mask) for source in range(lax.axis_size(axis))]
    return lax.ppermute(value, axis, pairs)


def body(queries, keys, values, near_blocks, near_count, head_scale, gain, cotangent):
    tok_rows = queries.shape[0]
    local_cols = queries.shape[1]
    heads_here = local_cols // HEAD_SIZE
    width = HEADS * HEAD_SIZE
    ctx_count = lax.axis_size("ctx")
    device = lax.axis_index("ctx")
    blocks_here = tok_rows // BLOCK_TOKENS
    margin = RB * BLOCK_TOKENS
    extended = blocks_here + 2 * RB
    columns = 2 * local_cols
    softmax_scale = 1.0 / math.sqrt(HEAD_SIZE)
    pair = jnp.concatenate([keys, values], axis=1)
    padded = padded_2(pair, (("ctx", 0),), margin)
    first_block = device * blocks_here - RB
    select = (near_blocks - first_block)[:, :, None] == jnp.arange(extended, dtype=jnp.int32)[
        None, None, :
    ]
    select_flat = select.reshape(blocks_here * NEAR_SLOTS, extended)
    near_pair = jnp.dot(
        select_flat.astype(jnp.bfloat16),
        padded.reshape(extended, BLOCK_TOKENS * columns),
        preferred_element_type=jnp.float32,
    )
    near_pair = near_pair.astype(jnp.bfloat16).reshape(
        blocks_here, NEAR_SLOTS, BLOCK_TOKENS, columns
    )
    valid = jnp.arange(NEAR_SLOTS, dtype=jnp.int32)[None, :] < near_count[:, None]
    key_mask = jnp.repeat(valid, BLOCK_TOKENS, axis=1)[:, None, :]
    factors = [2 ** (level_idx + 1) for level_idx in range(LEV)]
    groups = [min(2 ** (level_idx + 1), ctx_count) for level_idx in range(LEV)]
    pooled = [
        pair.astype(jnp.float32)
        .reshape(tok_rows // factors[level_idx], factors[level_idx], columns)
        .mean(axis=1)
        .astype(jnp.bfloat16)
        for level_idx in range(LEV)
    ]
    steps_count = max(groups).bit_length() - 1
    q_global = device * tok_rows + jnp.arange(tok_rows, dtype=jnp.int32)
    far_masks = []
    for level_idx in range(LEV):
        span_here = groups[level_idx] * tok_rows
        rows_level = span_here // factors[level_idx]
        group_first = device // groups[level_idx] * span_here
        key_first = group_first + jnp.arange(rows_level, dtype=jnp.int32) * factors[level_idx]
        keep = jnp.abs(key_first[None, :] // BLOCK_TOKENS - q_global[:, None] // BLOCK_TOKENS) > RB
        if level_idx > 0:
            prior = groups[level_idx - 1] * tok_rows
            keep = keep & (key_first[None, :] // prior != q_global[:, None] // prior)
        far_masks.append(keep)
    group_pair = list(pooled)
    shared = [level_idx for level_idx in range(LEV) if groups[level_idx] > 1]
    packed = jnp.concatenate([pooled[level_idx] for level_idx in shared], axis=0)
    everyone = lax.all_gather(packed, "ctx", axis=0, tiled=True).reshape(
        ctx_count, packed.shape[0], columns
    )
    offset = 0
    for level_idx in shared:
        count_rows = pooled[level_idx].shape[0]
        piece = everyone[:, offset : offset + count_rows]
        group_start = device // groups[level_idx] * groups[level_idx]
        chosen = lax.dynamic_slice_in_dim(piece, group_start, groups[level_idx], 0)
        group_pair[level_idx] = chosen.reshape(groups[level_idx] * count_rows, columns)
        offset = offset + count_rows
    saved = []
    attn_list = []
    for head_idx in range(heads_here):
        k_cols = slice(head_idx * HEAD_SIZE, (head_idx + 1) * HEAD_SIZE)
        v_cols = slice((heads_here + head_idx) * HEAD_SIZE, (heads_here + head_idx + 1) * HEAD_SIZE)
        q_head = queries[:, k_cols]
        query_blocks = q_head.reshape(blocks_here, BLOCK_TOKENS, HEAD_SIZE)
        near_key_rows = near_pair[:, :, :, k_cols].reshape(
            blocks_here, NEAR_SLOTS * BLOCK_TOKENS, HEAD_SIZE
        )
        near_value_rows = near_pair[:, :, :, v_cols].reshape(
            blocks_here, NEAR_SLOTS * BLOCK_TOKENS, HEAD_SIZE
        )
        near_score_rows = (
            jnp.einsum(
                "mne,mge->mng", query_blocks, near_key_rows, preferred_element_type=jnp.float32
            )
            * softmax_scale
        )
        near_score_rows = jnp.where(key_mask, near_score_rows, NEG_BIG)
        top = jnp.max(near_score_rows, axis=2).reshape(tok_rows)
        coarse_k = [group_pair[level_idx][:, k_cols] for level_idx in range(LEV)]
        coarse_v = [group_pair[level_idx][:, v_cols] for level_idx in range(LEV)]
        s_far = []
        for level_idx in range(LEV):
            scores = (
                jnp.einsum(
                    "td,kd->tk", q_head, coarse_k[level_idx], preferred_element_type=jnp.float32
                )
                * softmax_scale
                + (level_idx + 1) * LOG_TWO
            )
            scores = jnp.where(far_masks[level_idx], scores, NEG_BIG)
            s_far.append(scores)
            top = jnp.maximum(top, jnp.max(scores, axis=1))
        p_near = jnp.where(
            key_mask, jnp.exp(near_score_rows - top.reshape(blocks_here, BLOCK_TOKENS, 1)), 0.0
        )
        total = jnp.sum(p_near, axis=2).reshape(tok_rows)
        p_far = []
        for level_idx in range(LEV):
            exps = jnp.where(far_masks[level_idx], jnp.exp(s_far[level_idx] - top[:, None]), 0.0)
            p_far.append(exps)
            total = total + jnp.sum(exps, axis=1)
        prob_near = p_near / total.reshape(blocks_here, BLOCK_TOKENS, 1)
        near_weight_rows = prob_near.astype(jnp.bfloat16)
        attention_output = jnp.einsum(
            "itp,ipc->itc", near_weight_rows, near_value_rows, preferred_element_type=jnp.float32
        ).reshape(tok_rows, HEAD_SIZE)
        prob_far = []
        weight_far = []
        for level_idx in range(LEV):
            probs = p_far[level_idx] / total[:, None]
            weights_bf = probs.astype(jnp.bfloat16)
            prob_far.append(probs)
            weight_far.append(weights_bf)
            attention_output = attention_output + jnp.dot(
                weights_bf, coarse_v[level_idx], preferred_element_type=jnp.float32
            )
        attn_list.append(attention_output)
        saved.append(
            (
                q_head,
                query_blocks,
                near_key_rows,
                near_value_rows,
                prob_near,
                near_weight_rows,
                coarse_k,
                coarse_v,
                prob_far,
                weight_far,
            )
        )
    scaled = jnp.concatenate(
        [attn_list[head_idx] * head_scale[head_idx] for head_idx in range(heads_here)], axis=1
    )
    squares = lax.psum(jnp.sum(scaled * scaled, axis=1), "head")
    inv = lax.rsqrt(squares / width + NORM_EPS)
    mixed = (scaled * inv[:, None] * gain[None, :]).astype(jnp.bfloat16)
    back = cotangent.astype(jnp.float32) * gain[None, :]
    inner = lax.psum(jnp.sum(back * scaled, axis=1), "head")
    d_scaled = inv[:, None] * (back - scaled * (inv * inv * inner / width)[:, None])
    grad_q_list = []
    near_dk = []
    near_dv = []
    far_dk = [[] for level_idx in range(LEV)]
    far_dv = [[] for level_idx in range(LEV)]
    for head_idx in range(heads_here):
        (
            q_head,
            query_blocks,
            near_key_rows,
            near_value_rows,
            prob_near,
            near_weight_rows,
            coarse_k,
            coarse_v,
            prob_far,
            weight_far,
        ) = saved[head_idx]
        d_out = (
            d_scaled[:, head_idx * HEAD_SIZE : (head_idx + 1) * HEAD_SIZE] * head_scale[head_idx]
        ).astype(jnp.bfloat16)
        delta = jnp.sum(d_out.astype(jnp.float32) * attn_list[head_idx], axis=1)
        block_gradient = d_out.reshape(blocks_here, BLOCK_TOKENS, HEAD_SIZE)
        near_prob_gradient = jnp.einsum(
            "mne,mge->mng", block_gradient, near_value_rows, preferred_element_type=jnp.float32
        )
        near_score_gradient = (
            prob_near * (near_prob_gradient - delta.reshape(blocks_here, BLOCK_TOKENS, 1))
        ).astype(jnp.bfloat16)
        query_gradient = jnp.einsum(
            "itp,ipc->itc", near_score_gradient, near_key_rows, preferred_element_type=jnp.float32
        ).reshape(tok_rows, HEAD_SIZE)
        near_dk.append(
            jnp.einsum(
                "ail,aiz->alz",
                near_score_gradient,
                query_blocks,
                preferred_element_type=jnp.float32,
            )
            * softmax_scale
        )
        near_dv.append(
            jnp.einsum(
                "ail,aiz->alz", near_weight_rows, block_gradient, preferred_element_type=jnp.float32
            )
        )
        for level_idx in range(LEV):
            dp_far = jnp.einsum(
                "td,kd->tk", d_out, coarse_v[level_idx], preferred_element_type=jnp.float32
            )
            ds_far = (prob_far[level_idx] * (dp_far - delta[:, None])).astype(jnp.bfloat16)
            query_gradient = query_gradient + jnp.dot(
                ds_far, coarse_k[level_idx], preferred_element_type=jnp.float32
            )
            far_dk[level_idx].append(
                jnp.einsum("tk,td->kd", ds_far, q_head, preferred_element_type=jnp.float32)
                * softmax_scale
            )
            far_dv[level_idx].append(
                jnp.einsum(
                    "tk,td->kd", weight_far[level_idx], d_out, preferred_element_type=jnp.float32
                )
            )
        grad_q_list.append(query_gradient * softmax_scale)
    contrib = jnp.concatenate(near_dk + near_dv, axis=2).reshape(
        blocks_here * NEAR_SLOTS, BLOCK_TOKENS * columns
    )
    spread_ext = jnp.einsum(
        "xe,xc->ec", select_flat.astype(jnp.float32), contrib, precision=lax.Precision.HIGHEST
    )
    spread_ext = spread_ext.reshape(extended * BLOCK_TOKENS, columns)
    lower_rim = spread_ext[:margin]
    own_rows = spread_ext[margin : margin + tok_rows]
    upper_rim = spread_ext[margin + tok_rows :]
    from_above = passed_along(lower_rim.astype(jnp.bfloat16), "ctx", -1).astype(lower_rim.dtype)
    from_below = passed_along(upper_rim.astype(jnp.bfloat16), "ctx", 1).astype(upper_rim.dtype)
    grad_pair = own_rows + from_above + from_below
    far_grad = [
        jnp.concatenate(far_dk[level_idx] + far_dv[level_idx], axis=1) for level_idx in range(LEV)
    ]
    for bit_idx in reversed(range(steps_count)):
        active = [level_idx for level_idx in range(LEV) if groups[level_idx] > 2**bit_idx]
        upper_half = device // 2**bit_idx % 2 == 1
        sends = []
        keeps = []
        for level_idx in active:
            half_rows = far_grad[level_idx].shape[0] // 2
            lower_part = far_grad[level_idx][:half_rows]
            upper_part = far_grad[level_idx][half_rows:]
            keeps.append(jnp.where(upper_half, upper_part, lower_part))
            sends.append(jnp.where(upper_half, lower_part, upper_part))
        received = from_partner(shortened(jnp.concatenate(sends, axis=0)), "ctx", bit_idx)
        offset = 0
        for position, level_idx in enumerate(active):
            half_rows = keeps[position].shape[0]
            far_grad[level_idx] = keeps[position] + received[offset : offset + half_rows]
            offset = offset + half_rows
    for level_idx in range(LEV):
        factor = factors[level_idx]
        rows_level = far_grad[level_idx].shape[0]
        expanded = jnp.broadcast_to(
            (far_grad[level_idx] / factor)[:, None, :], (rows_level, factor, columns)
        )
        grad_pair = grad_pair + expanded.reshape(tok_rows, columns)
    grad_queries = jnp.concatenate(grad_q_list, axis=1).astype(jnp.bfloat16)
    grad_keys = grad_pair[:, :local_cols].astype(jnp.bfloat16)
    grad_values = grad_pair[:, local_cols:].astype(jnp.bfloat16)
    return (mixed, grad_queries, grad_keys, grad_values)


def solution(mesh):
    return jax.shard_map(
        body,
        mesh=mesh,
        in_specs=(
            P("ctx", "head"),
            P("ctx", "head"),
            P("ctx", "head"),
            P("ctx", None),
            P("ctx"),
            P("head"),
            P("head"),
            P("ctx", "head"),
        ),
        out_specs=(P("ctx", "head"), P("ctx", "head"), P("ctx", "head"), P("ctx", "head")),
        check_vma=False,
    )
```

profile of v0, /device:TPU:1, one launch (start us, length us, event | category | flops | bytes accessed | tf_op | source)
XLA Modules:
  0.0 259.7 jit_solution(10416025845603578630)
XLA Ops:
  13.6 4.5 %collective-permute-start = (bf16[256,512]{1,0:T(8,128)(2,1)S(1)}, bf16[256,512]{1,0:T(8,128)(2,1)S(1)}, u32[]{:S(2)}, u32[]{:S(2)}) collective-permute-start(bf16[256,512]{1,0:T(8,128)(2,1)S(1)} %constant_dynamic-update-slice_fusion), channel_id=1, source_target_pairs={{0,16},{16,32},{32,48},{48,64},{64,80},{80,96},{96,112},{112,128},... | collective-permute-start | bytes 786440 | tf_op jit(solution)/shard_map/ppermute | solution.py:29
  18.1 5.6 %collective-permute-start.1 = (bf16[256,512]{1,0:T(8,128)(2,1)S(1)}, bf16[256,512]{1,0:T(8,128)(2,1)S(1)}, u32[]{:S(2)}, u32[]{:S(2)}) collective-permute-start(bf16[256,512]{1,0:T(8,128)(2,1)S(1)} %constant_dynamic-update-slice_fusion), channel_id=1, source_target_pairs={{16,0},{32,16},{48,32},{64,48},{80,64},{96,80},{112,96},{128,112},... | collective-permute-start | bytes 786440 | tf_op jit(solution)/shard_map/ppermute | solution.py:31
  28.6 1.1 fusion.272
  30.2 56.8 %all-gather.2.cloned.1.call-done = bf16[7936,512]{1,0:T(8,128)(2,1)} async-done(((bf16[248,512]{1,0:T(8,128)(2,1)}), bf16[7936,512]{1,0:T(8,128)(2,1)}) %all-gather.2.cloned.1.call-update) | async-done | bytes 8126480 | tf_op jit(solution)/shard_map/all_gather | solution.py:112
  87.0 2.6 %slice.349 = bf16[32,128,512]{2,1,0:T(8,128)(2,1)S(1)} slice(bf16[32,248,512]{2,1,0:T(8,128)(2,1)} %bitcast.285), slice={[0:32], [0:128], [0:512]} | slice | bytes 8388608 | tf_op jit(solution)/shard_map/slice | solution.py:118
  89.7 1.8 slice.351
  91.5 1.3 slice.353
  92.8 1.1 slice.355
  101.5 1.1 fusion.101
  102.6 1.7 copy.148
  104.3 1.3 convolution_add_fusion.19
  105.6 1.3 convolution_add_fusion.18
  109.0 1.1 fusion.97
  110.1 1.7 copy.267
  111.8 1.2 convolution_add_fusion.14
  113.1 1.3 convolution_add_fusion.13
  115.9 1.5 broadcast_multiply_fusion.1
  117.5 1.6 broadcast_multiply_fusion
  119.8 25.6 %all-reduce = (f32[256]{0:T(256)}, f32[256]{0:T(256)}) all-reduce(f32[256]{0:T(256)} %get-tuple-element.21, f32[256]{0:T(256)} %get-tuple-element.20), channel_id=1, replica_groups=mesh['ctx'=32,'head'=16] {'head'}, use_global_device_ids=true, to_apply=%region_30.31 | all-reduce | flops 512 | bytes 4096 | tf_op jit(solution)/shard_map/psum | solution.py:200
  146.2 1.8 subtract_multiply_fusion
  147.9 2.2 multiply_reduce_fusion.3
  150.2 1.9 fusion.130
  152.1 1.7 fusion.127
  172.3 4.4 %collective-permute-start.4 = (bf16[128,512]{1,0:T(8,128)(2,1)}, bf16[128,512]{1,0:T(8,128)(2,1)}, u32[]{:S(2)}, u32[]{:S(2)}) collective-permute-start(bf16[128,512]{1,0:T(8,128)(2,1)} %select_convert_fusion), channel_id=1, source_target_pairs={{0,256},{16,272},{32,288},{48,304},{64,320},{80,336},{96,352},{112... | collective-permute-start | bytes 393224 | tf_op jit(solution)/shard_map/ppermute | solution.py:55
  180.2 1.7 reshape.810
  181.9 2.8 %fusion.288 = (bf16[6,65536]{1,0:T(8,128)(2,1)S(1)}, f32[6,65536]{1,0:T(8,128)S(1)}) fusion(f32[8,65536]{1,0:T(8,128)} %reshape.810, s32[8]{0:T(128)S(1)} %copy-done.132), kind=kOutput, calls=%fused_computation.486 | convolution fusion | flops 38142000 | bytes 4456480 | tf_op jit(solution)/shard_map/xe,xc->ec/dot_general | solution.py:273
  186.0 9.1 %collective-permute-start.2 = (bf16[256,512]{1,0:T(8,128)(2,1)}, bf16[256,512]{1,0:T(8,128)(2,1)}, u32[]{:S(2)}, u32[]{:S(2)}) collective-permute-start(bf16[256,512]{1,0:T(8,128)(2,1)} %convert_element_type.240), channel_id=1, source_target_pairs={{16,0},{32,16},{48,32},{64,48},{80,64},{96,80},{112,96},{128,112},... | collective-permute-start | bytes 786440 | tf_op jit(solution)/shard_map/ppermute | solution.py:41
  196.0 2.1 collective-permute-start.3
  198.1 1.1 convolution_add_fusion.9
  199.3 1.2 convolution_add_fusion.8
  200.5 1.1 convolution_add_fusion.7
  201.6 1.1 convolution_add_fusion.6
  202.8 1.2 convolution_add_fusion.4
  204.0 1.1 convolution_add_fusion.3
  205.1 1.8 convolution_add_fusion.2
  207.3 1.1 convert_add_fusion.3
  208.5 2.2 collective-permute-start.5
  210.7 4.8 %collective-permute-done.5 = bf16[192,512]{1,0:T(8,128)(2,1)S(1)} collective-permute-done((bf16[192,512]{1,0:T(8,128)(2,1)S(1)}, bf16[192,512]{1,0:T(8,128)(2,1)S(1)}, u32[]{:S(2)}, u32[]{:S(2)}) %collective-permute-start.5) | collective-permute-done | bytes 196640 | tf_op jit(solution)/shard_map/ppermute | solution.py:55
  215.7 5.5 %collective-permute-start.6 = (bf16[224,512]{1,0:T(8,128)(2,1)S(1)}, bf16[224,512]{1,0:T(8,128)(2,1)S(1)}, u32[]{:S(2)}, u32[]{:S(2)}) collective-permute-start(bf16[224,512]{1,0:T(8,128)(2,1)S(1)} %pad_maximum_fusion.9), channel_id=1, source_target_pairs={{0,64},{16,80},{32,96},{48,112},{64,0},{80,16},{96,32},{112,48},{1... | collective-permute-start | bytes 688136 | tf_op jit(solution)/shard_map/ppermute | solution.py:55
  221.9 3.7 %collective-permute-done.6 = bf16[224,512]{1,0:T(8,128)(2,1)S(1)} collective-permute-done((bf16[224,512]{1,0:T(8,128)(2,1)S(1)}, bf16[224,512]{1,0:T(8,128)(2,1)S(1)}, u32[]{:S(2)}, u32[]{:S(2)}) %collective-permute-start.6) | collective-permute-done | bytes 229408 | tf_op jit(solution)/shard_map/ppermute | solution.py:55
  226.5 4.9 %collective-permute-start.7 = (bf16[240,512]{1,0:T(8,128)(2,1)}, bf16[240,512]{1,0:T(8,128)(2,1)}, u32[]{:S(2)}, u32[]{:S(2)}) collective-permute-start(bf16[240,512]{1,0:T(8,128)(2,1)} %pad_maximum_fusion.8), channel_id=1, source_target_pairs={{0,32},{16,48},{32,0},{48,16},{64,96},{80,112},{96,64},{112,80},{1... | collective-permute-start | bytes 737288 | tf_op jit(solution)/shard_map/ppermute | solution.py:55
  231.5 1.7 fusion.61
  234.3 1.5 slice.299
  235.8 1.7 copy.210
  237.5 1.2 convolution_add_fusion.1
  244.7 3.4 %collective-permute-start.8 = (bf16[248,512]{1,0:T(8,128)(2,1)}, bf16[248,512]{1,0:T(8,128)(2,1)S(1)}, u32[]{:S(2)}, u32[]{:S(2)}) collective-permute-start(bf16[248,512]{1,0:T(8,128)(2,1)} %constant_dynamic-update-slice_fusion.4), channel_id=1, source_target_pairs={{0,16},{16,0},{32,48},{48,32},{64,80},{80,64},{96,112},{112,96},{1... | collective-permute-start | bytes 761864 | tf_op jit(solution)/shard_map/ppermute | solution.py:55
  248.1 1.1 fusion.60
  250.9 1.3 fusion.62
  (459 shorter events, 58.3 us)
Async XLA Ops:
  7.2 79.8 %all-gather.2.cloned.1.call-start = ((), (), s32[]{:S(2)}) async-start(), calls=%async_computation | async-start | bytes 8380416 | tf_op jit(solution)/shard_map/all_gather | solution.py:112
  8.3 17.3 %copy-start.130 = (f32[2]{0:T(128)S(1)}, f32[2]{0:T(128)}, u32[]{:S(2)}) copy-start(f32[2]{0:T(128)} %param.13) | copy-start | bytes 28
  8.3 17.9 %copy-start.146 = (s32[2]{0:T(128)S(1)}, s32[2]{0:T(128)}, u32[]{:S(2)}) copy-start(s32[2]{0:T(128)} %param.12) | copy-start | bytes 28
  8.3 18.1 %copy-start.145 = (s32[2,4]{1,0:T(2,128)S(1)}, s32[2,4]{1,0:T(2,128)}, u32[]{:S(2)}) copy-start(s32[2,4]{1,0:T(2,128)} %param.11) | copy-start | bytes 100
  9.2 17.3 %copy-start.71 = (bf16[256,256]{1,0:T(8,128)(2,1)S(1)}, bf16[256,256]{1,0:T(8,128)(2,1)}, u32[]{:S(2)}) copy-start(bf16[256,256]{1,0:T(8,128)(2,1)} %param.15) | copy-start | bytes 393220
  10.3 16.5 %copy-start = (bf16[256,256]{1,0:T(8,128)(2,1)S(1)}, bf16[256,256]{1,0:T(8,128)(2,1)}, u32[]{:S(2)}) copy-start(bf16[256,256]{1,0:T(8,128)(2,1)} %param.8) | copy-start | bytes 393220
  13.6 13.2 %collective-permute-start = (bf16[256,512]{1,0:T(8,128)(2,1)S(1)}, bf16[256,512]{1,0:T(8,128)(2,1)S(1)}, u32[]{:S(2)}, u32[]{:S(2)}) collective-permute-start(bf16[256,512]{1,0:T(8,128)(2,1)S(1)} %constant_dynamic-update-slice_fusion), channel_id=1, source_target_pairs={{0,16},{16,32},{32,48},{48,64},{64,80},{80,96},{96,112},{112,128},... | collective-permute-start | bytes 786440 | tf_op jit(solution)/shard_map/ppermute | solution.py:29
  18.1 8.7 %collective-permute-start.1 = (bf16[256,512]{1,0:T(8,128)(2,1)S(1)}, bf16[256,512]{1,0:T(8,128)(2,1)S(1)}, u32[]{:S(2)}, u32[]{:S(2)}) collective-permute-start(bf16[256,512]{1,0:T(8,128)(2,1)S(1)} %constant_dynamic-update-slice_fusion), channel_id=1, source_target_pairs={{16,0},{32,16},{48,32},{64,48},{80,64},{96,80},{112,96},{128,112},... | collective-permute-start | bytes 786440 | tf_op jit(solution)/shard_map/ppermute | solution.py:31
  23.7 73.8 %copy-start.81 = (s32[256]{0:T(256)}, s32[256]{0:T(256)S(1)}, u32[]{:S(2)}) copy-start(s32[256]{0:T(256)S(1)} %and_select_fusion.12) | copy-start | bytes 3076
  23.8 72.0 %copy-start.86 = (s32[256]{0:T(256)}, s32[256]{0:T(256)S(1)}, u32[]{:S(2)}) copy-start(s32[256]{0:T(256)S(1)} %get-tuple-element.101) | copy-start | bytes 3076
  23.8 72.6 %copy-start.98 = (s32[256]{0:T(256)}, s32[256]{0:T(256)S(1)}, u32[]{:S(2)}) copy-start(s32[256]{0:T(256)S(1)} %get-tuple-element.100) | copy-start | bytes 3076
  23.8 72.5 %copy-start.101 = (s32[256]{0:T(256)}, s32[256]{0:T(256)S(1)}, u32[]{:S(2)}) copy-start(s32[256]{0:T(256)S(1)} %get-tuple-element.98) | copy-start | bytes 3076
  23.8 72.5 %copy-start.104 = (s32[256]{0:T(256)}, s32[256]{0:T(256)S(1)}, u32[]{:S(2)}) copy-start(s32[256]{0:T(256)S(1)} %get-tuple-element.99) | copy-start | bytes 3076
  25.0 70.7 %copy-start.111 = (s32[256]{0:T(256)}, s32[256]{0:T(256)S(1)}, u32[]{:S(2)}) copy-start(s32[256]{0:T(256)S(1)} %get-tuple-element.102) | copy-start | bytes 3076
  25.0 70.7 %copy-start.114 = (s32[256]{0:T(256)}, s32[256]{0:T(256)S(1)}, u32[]{:S(2)}) copy-start(s32[256]{0:T(256)S(1)} %get-tuple-element.103) | copy-start | bytes 3076
  26.4 68.8 %copy-start.133 = (s32[256]{0:T(256)}, s32[256]{0:T(256)S(1)}, u32[]{:S(2)}) copy-start(s32[256]{0:T(256)S(1)} %and_select_fusion.13) | copy-start | bytes 3076
  94.9 63.1 %copy-start.10 = (bf16[256,512]{1,0:T(8,128)(2,1)}, bf16[256,512]{1,0:T(8,128)(2,1)S(1)}, u32[]{:S(2)}) copy-start(bf16[256,512]{1,0:T(8,128)(2,1)S(1)} %slice_bitcast_fusion) | copy-start | bytes 786436
  94.9 68.7 %copy-start.7 = (bf16[2,128,512]{2,1,0:T(8,128)(2,1)}, bf16[2,128,512]{2,1,0:T(8,128)(2,1)S(1)}, u32[]{:S(2)}) copy-start(bf16[2,128,512]{2,1,0:T(8,128)(2,1)S(1)} %constant_dynamic-slice_fusion.3) | copy-start | bytes 786436
  95.2 16.6 %copy-start.40 = (f32[256,256]{0,1:T(8,128)}, f32[256,256]{0,1:T(8,128)S(1)}, u32[]{:S(2)}) copy-start(f32[256,256]{0,1:T(8,128)S(1)} %get-tuple-element.83) | copy-start | bytes 786436
  95.4 65.3 %copy-start.8 = (bf16[4,64,512]{2,1,0:T(8,128)(2,1)}, bf16[4,64,512]{2,1,0:T(8,128)(2,1)S(1)}, u32[]{:S(2)}) copy-start(bf16[4,64,512]{2,1,0:T(8,128)(2,1)S(1)} %constant_dynamic-slice_fusion.2) | copy-start | bytes 786436
  96.1 60.1 %copy-start.9 = (bf16[8,32,512]{2,1,0:T(8,128)(2,1)}, bf16[8,32,512]{2,1,0:T(8,128)(2,1)S(1)}, u32[]{:S(2)}) copy-start(bf16[8,32,512]{2,1,0:T(8,128)(2,1)S(1)} %constant_dynamic-slice_fusion.1) | copy-start | bytes 786436
  96.7 104.9 %copy-start.6 = (bf16[16,16,512]{2,1,0:T(8,128)(2,1)}, bf16[16,16,512]{2,1,0:T(8,128)(2,1)S(1)}, u32[]{:S(2)}) copy-start(bf16[16,16,512]{2,1,0:T(8,128)(2,1)S(1)} %constant_dynamic-slice_fusion) | copy-start | bytes 786436
  117.5 28.7 %copy-start.28 = (f32[256,128]{0,1:T(8,128)}, f32[256,128]{0,1:T(8,128)S(1)}, u32[]{:S(2)}) copy-start(f32[256,128]{0,1:T(8,128)S(1)} %get-tuple-element.88) | copy-start | bytes 393220
  119.1 27.1 %copy-start.29 = (f32[256,128]{0,1:T(8,128)}, f32[256,128]{0,1:T(8,128)S(1)}, u32[]{:S(2)}) copy-start(f32[256,128]{0,1:T(8,128)S(1)} %get-tuple-element.86) | copy-start | bytes 393220
  155.9 11.9 %copy-start.22 = (bf16[256,256]{0,1:T(8,128)(2,1)}, bf16[256,256]{0,1:T(8,128)(2,1)S(1)}, u32[]{:S(2)}) copy-start(bf16[256,256]{0,1:T(8,128)(2,1)S(1)} %fusion.50) | copy-start | bytes 393220
  156.2 13.3 %copy-start.21 = (bf16[256,256]{0,1:T(8,128)(2,1)}, bf16[256,256]{0,1:T(8,128)(2,1)S(1)}, u32[]{:S(2)}) copy-start(bf16[256,256]{0,1:T(8,128)(2,1)S(1)} %fusion.51) | copy-start | bytes 393220
  156.4 12.2 %copy-start.19 = (bf16[256,256]{0,1:T(8,128)(2,1)}, bf16[256,256]{0,1:T(8,128)(2,1)S(1)}, u32[]{:S(2)}) copy-start(bf16[256,256]{0,1:T(8,128)(2,1)S(1)} %fusion.55) | copy-start | bytes 393220
  157.2 13.2 %copy-start.16 = (bf16[256,256]{0,1:T(8,128)(2,1)}, bf16[256,256]{0,1:T(8,128)(2,1)S(1)}, u32[]{:S(2)}) copy-start(bf16[256,256]{0,1:T(8,128)(2,1)S(1)} %fusion.56) | copy-start | bytes 393220
  158.0 13.2 %copy-start.17 = (bf16[256,256]{0,1:T(8,128)(2,1)}, bf16[256,256]{0,1:T(8,128)(2,1)S(1)}, u32[]{:S(2)}) copy-start(bf16[256,256]{0,1:T(8,128)(2,1)S(1)} %fusion.52) | copy-start | bytes 393220
  158.7 12.6 %copy-start.14 = (bf16[256,256]{0,1:T(8,128)(2,1)}, bf16[256,256]{0,1:T(8,128)(2,1)S(1)}, u32[]{:S(2)}) copy-start(bf16[256,256]{0,1:T(8,128)(2,1)S(1)} %fusion.57) | copy-start | bytes 393220
  160.8 15.9 %copy-start.25 = (bf16[256,256]{0,1:T(8,128)(2,1)}, bf16[256,256]{0,1:T(8,128)(2,1)S(1)}, u32[]{:S(2)}) copy-start(bf16[256,256]{0,1:T(8,128)(2,1)S(1)} %fusion.49) | copy-start | bytes 393220
  161.5 16.0 %copy-start.23 = (bf16[256,256]{0,1:T(8,128)(2,1)}, bf16[256,256]{0,1:T(8,128)(2,1)S(1)}, u32[]{:S(2)}) copy-start(bf16[256,256]{0,1:T(8,128)(2,1)S(1)} %fusion.54) | copy-start | bytes 393220
  163.6 14.8 %copy-start.27 = (bf16[256,256]{0,1:T(8,128)(2,1)}, bf16[256,256]{0,1:T(8,128)(2,1)S(1)}, u32[]{:S(2)}) copy-start(bf16[256,256]{0,1:T(8,128)(2,1)S(1)} %fusion.48) | copy-start | bytes 393220
  163.8 15.4 %copy-start.26 = (bf16[256,256]{0,1:T(8,128)(2,1)}, bf16[256,256]{0,1:T(8,128)(2,1)S(1)}, u32[]{:S(2)}) copy-start(bf16[256,256]{0,1:T(8,128)(2,1)S(1)} %fusion.53) | copy-start | bytes 393220
  172.3 35.1 %collective-permute-start.4 = (bf16[128,512]{1,0:T(8,128)(2,1)}, bf16[128,512]{1,0:T(8,128)(2,1)}, u32[]{:S(2)}, u32[]{:S(2)}) collective-permute-start(bf16[128,512]{1,0:T(8,128)(2,1)} %select_convert_fusion), channel_id=1, source_target_pairs={{0,256},{16,272},{32,288},{48,304},{64,320},{80,336},{96,352},{112... | collective-permute-start | bytes 393224 | tf_op jit(solution)/shard_map/ppermute | solution.py:55
  184.6 13.4 %copy-start.12 = (f32[2,128,128]{2,1,0:T(8,128)S(1)}, f32[2,128,128]{2,1,0:T(8,128)}, u32[]{:S(2)}) copy-start(f32[2,128,128]{2,1,0:T(8,128)} %fusion.289) | copy-start | bytes 393220
  186.0 16.8 %copy-start.13 = (f32[2,128,128]{2,1,0:T(8,128)S(1)}, f32[2,128,128]{2,1,0:T(8,128)}, u32[]{:S(2)}) copy-start(f32[2,128,128]{2,1,0:T(8,128)} %fusion.290) | copy-start | bytes 393220
  186.0 64.9 %collective-permute-start.2 = (bf16[256,512]{1,0:T(8,128)(2,1)}, bf16[256,512]{1,0:T(8,128)(2,1)}, u32[]{:S(2)}, u32[]{:S(2)}) collective-permute-start(bf16[256,512]{1,0:T(8,128)(2,1)} %convert_element_type.240), channel_id=1, source_target_pairs={{16,0},{32,16},{48,32},{64,48},{80,64},{96,80},{112,96},{128,112},... | collective-permute-start | bytes 786440 | tf_op jit(solution)/shard_map/ppermute | solution.py:41
  196.0 54.8 %collective-permute-start.3 = (bf16[256,512]{1,0:T(8,128)(2,1)}, bf16[256,512]{1,0:T(8,128)(2,1)}, u32[]{:S(2)}, u32[]{:S(2)}) collective-permute-start(bf16[256,512]{1,0:T(8,128)(2,1)} %convert_element_type.242), channel_id=1, source_target_pairs={{0,16},{16,32},{32,48},{48,64},{64,80},{80,96},{96,112},{112,128},... | collective-permute-start | bytes 786440 | tf_op jit(solution)/shard_map/ppermute | solution.py:41
  208.5 7.1 %collective-permute-start.5 = (bf16[192,512]{1,0:T(8,128)(2,1)S(1)}, bf16[192,512]{1,0:T(8,128)(2,1)S(1)}, u32[]{:S(2)}, u32[]{:S(2)}) collective-permute-start(bf16[192,512]{1,0:T(8,128)(2,1)S(1)} %pad_maximum_fusion.10), channel_id=1, source_target_pairs={{0,128},{16,144},{32,160},{48,176},{64,192},{80,208},{96,224},{112... | collective-permute-start | bytes 589832 | tf_op jit(solution)/shard_map/ppermute | solution.py:55
  215.6 15.9 %copy-start.18 = (bf16[256,256]{0,1:T(8,128)(2,1)S(1)}, bf16[256,256]{0,1:T(8,128)(2,1)}, u32[]{:S(2)}) copy-start(bf16[256,256]{0,1:T(8,128)(2,1)} %copy-done.17) | copy-start | bytes 393220
  215.7 9.9 %collective-permute-start.6 = (bf16[224,512]{1,0:T(8,128)(2,1)S(1)}, bf16[224,512]{1,0:T(8,128)(2,1)S(1)}, u32[]{:S(2)}, u32[]{:S(2)}) collective-permute-start(bf16[224,512]{1,0:T(8,128)(2,1)S(1)} %pad_maximum_fusion.9), channel_id=1, source_target_pairs={{0,64},{16,80},{32,96},{48,112},{64,0},{80,16},{96,32},{112,48},{1... | collective-permute-start | bytes 688136 | tf_op jit(solution)/shard_map/ppermute | solution.py:55
  225.7 14.0 %copy-start.5 = (f32[64,512]{1,0:T(8,128)}, f32[64,512]{1,0:T(8,128)S(1)}, u32[]{:S(2)}) copy-start(f32[64,512]{1,0:T(8,128)S(1)} %convert_add_fusion.5) | copy-start | bytes 393220
  225.7 13.0 %copy-start.4 = (f32[256,512]{1,0:T(8,128)S(1)}, f32[256,512]{1,0:T(8,128)}, u32[]{:S(2)}) copy-start(f32[256,512]{1,0:T(8,128)} %copy-done.3) | copy-start | bytes 1572868
  226.5 12.2 %collective-permute-start.7 = (bf16[240,512]{1,0:T(8,128)(2,1)}, bf16[240,512]{1,0:T(8,128)(2,1)}, u32[]{:S(2)}, u32[]{:S(2)}) collective-permute-start(bf16[240,512]{1,0:T(8,128)(2,1)} %pad_maximum_fusion.8), channel_id=1, source_target_pairs={{0,32},{16,48},{32,0},{48,16},{64,96},{80,112},{96,64},{112,80},{1... | collective-permute-start | bytes 737288 | tf_op jit(solution)/shard_map/ppermute | solution.py:55
  234.3 13.8 %copy-start.15 = (bf16[256,256]{0,1:T(8,128)(2,1)S(1)}, bf16[256,256]{0,1:T(8,128)(2,1)}, u32[]{:S(2)}) copy-start(bf16[256,256]{0,1:T(8,128)(2,1)} %copy-done.14) | copy-start | bytes 393220
  234.3 14.9 %copy-start.66 = (bf16[256,128]{1,0:T(8,128)(2,1)S(1)}, bf16[256,128]{1,0:T(8,128)(2,1)}, u32[]{:S(2)}) copy-start(bf16[256,128]{1,0:T(8,128)(2,1)} %fusion.61) | copy-start | bytes 196612
  244.7 5.2 %collective-permute-start.8 = (bf16[248,512]{1,0:T(8,128)(2,1)}, bf16[248,512]{1,0:T(8,128)(2,1)S(1)}, u32[]{:S(2)}, u32[]{:S(2)}) collective-permute-start(bf16[248,512]{1,0:T(8,128)(2,1)} %constant_dynamic-update-slice_fusion.4), channel_id=1, source_target_pairs={{0,16},{16,0},{32,48},{48,32},{64,80},{80,64},{96,112},{112,96},{1... | collective-permute-start | bytes 761864 | tf_op jit(solution)/shard_map/ppermute | solution.py:55
  (110 other events, 407.6 us)
Sparse Core Ops, SparseCore 0:
  13.6 73.3 all-gather.1
where the time goes:
time: 261 us; the launch traced here: 260 us
  waiting for transfers between devices  65.4 us (25%)
  matrix products  55.1 us (21%)
  starting transfers between devices  41.8 us (16%)
  local copies, waits for them, and re-layouts  30.9 us (12%)
  blocking collectives  25.6 us (10%)
  other arithmetic  24.1 us (9%)
  between operations  16.8 us (6%)
    all_gather x1, waiting for transfers between devices, body(): lax.all_gather(packed, 'ctx', axis=0, tiled=True)  56.8 us
    psum x1, blocking collectives, body(): squares = lax.psum(jnp.sum(scaled * scaled, axis=1), 'head')  25.6 us
    ppermute x5, starting transfers between devices, from_partner(): return lax.ppermute(value, axis, pairs)  20.5 us
    dot_general x10, matrix products, body(): jnp.dot(ds_far, coarse_k[level_idx], preferred_element_type=jnp.float32)  12.6 us
    dot_general x10, matrix products, body(): jnp.dot(weights_bf, coarse_v[level_idx], preferred_element_type=jnp.float32)  11.6 us
    ppermute x2, starting transfers between devices, passed_along(): return lax.ppermute(value, axis, pairs)  11.2 us
    dot_general x10, matrix products, body(): jnp.einsum('tk,td->kd', weight_far[level_idx], d_out, preferred_element_t...  9.72 us
    ppermute x5, waiting for transfers between devices, from_partner(): return lax.ppermute(value, axis, pairs)  8.53 us
  transfers between devices with their start and end apart: 10, of which 3 were waited for; matrix products, arithmetic and copies ran while one was open for 17% of the time, Pallas kernels for 0%

commit v1 on v0

v1 whole, which is shorter than its diff:
```python
import functools
import math

import jax
import jax.numpy as jnp
from jax import lax
from jax.experimental import pallas as pl
from jax.experimental.pallas import tpu as pltpu
from jax.sharding import PartitionSpec as P

HS = 128
BT = 128
SLOTS = 4
NEG_BIG = -1e30
NORM_EPS = 1e-05
LOG2E = 1.4426950408889634
SCALE = 1.0 / math.sqrt(HS)
TOK = 256
COLS = 512
NEAR = 768
ROWS = 1408
COARSE = ROWS - NEAR
F32 = jnp.float32
BF16 = jnp.bfloat16


def dot(a, b, ca, cb):
    return lax.dot_general(
        a, b, (((ca,), (cb,)), ((), ())), preferred_element_type=F32
    )


def iota(shape, dim):
    return lax.broadcasted_iota(jnp.int32, shape, dim)


def pool_matrix(rows, level):
    hit = (iota((rows, TOK), 1) >> level) == iota((rows, TOK), 0)
    return jnp.where(hit, 2.0**-level, 0.0)


def kernel(
    n_ctx, n_head,
    q_hbm, k_hbm, v_hbm, nb_ref, nc_ref, hs_ref, gain_ref, cot_hbm,
    mixed_hbm, gq_hbm, gk_hbm, gv_hbm,
    kall, qv, cotv, pool, pool5, buf5, ps_own, ps_buf, cbias, back,
    pt, dst, cg, ext, c_send, c_recv, rim_out, rim_in, csum, csum5, ret, ret5,
    mixed_v, gq_v, gk_v, gv_v,
    ld_sem, out_sem, pool_send, pool_recv, fwd_send, fwd_recv, near_send, near_recv,
    ps_sem, cp_sem, rim_send, rim_recv, ret_send, ret_recv,
):
    d = lax.axis_index("ctx")
    z = lax.axis_index("head")
    n_chip = n_ctx // 2
    chip = lax.div(d, 2)
    core = lax.rem(d, 2)
    partner = chip * 2 + 1 - core
    other = lax.rem(d + n_ctx - 1 + 2 * core, n_ctx)
    width = float(n_head * 2 * HS)

    barrier = pltpu.get_barrier_semaphore()

    def hello(ctx, head):
        pl.semaphore_signal(
            barrier, inc=1, device_id=(ctx, head), device_id_type=pl.DeviceIdType.MESH
        )

    for m in range(1, n_head):
        hello(d, lax.rem(z + m, n_head))
    for m in range(1, n_chip):
        hello(lax.rem(chip + m, n_chip) * 2 + core, z)
    hello(other, z)
    hello(partner, z)

    def remote(src, dst_ref, ssem, rsem, ctx, head):
        return pltpu.make_async_remote_copy(
            src_ref=src, dst_ref=dst_ref, send_sem=ssem, recv_sem=rsem,
            device_id=(ctx, head), device_id_type=pl.DeviceIdType.MESH,
        )

    def wait_bytes(ref, sem):
        pltpu.make_async_copy(ref, ref, sem).wait()

    loads = [
        pltpu.make_async_copy(k_hbm, kall.at[pl.ds(TOK, TOK), pl.ds(0, 256)], ld_sem.at[0]),
        pltpu.make_async_copy(v_hbm, kall.at[pl.ds(TOK, TOK), pl.ds(256, 256)], ld_sem.at[1]),
        pltpu.make_async_copy(q_hbm, qv, ld_sem.at[2]),
        pltpu.make_async_copy(cot_hbm, cotv, ld_sem.at[3]),
    ]
    for load in loads:
        load.start()
    loads[0].wait()
    loads[1].wait()

    pm = jnp.concatenate(
        [pool_matrix(64, 2), pool_matrix(32, 3), pool_matrix(16, 4), pool_matrix(8, 5),
         jnp.zeros((8, TOK), F32)], axis=0,
    ).astype(BF16)
    pooled = dot(pm, kall[TOK : 2 * TOK, :], 1, 0)
    pool[...] = pooled[0:112].astype(BF16)
    pool5[...] = jnp.concatenate([pooled[112:120, 0:256], pooled[112:120, 256:512]], axis=0).astype(BF16)

    pl.semaphore_wait(barrier, n_head - 1 + n_chip - 1 + 2)

    def level_peers(li):
        c = 1 << li
        half = lax.div(chip, c)
        base = (half + 1 - 2 * lax.rem(half, 2)) * c
        return c, 64 >> li, base, lax.rem(chip, c)

    pool_off = (0, 64, 96)
    for li in range(4):
        c, n, base, pos = level_peers(li)
        for j in range(c):
            if li < 3:
                src = pool.at[pl.ds(pool_off[li], n)]
                row = pl.multiple_of(NEAR + 128 * (li + 1) + core * 64 + pos * n, 16)
                dst_ref = kall.at[pl.ds(row, n)]
            else:
                src = pool5
                dst_ref = buf5.at[core * 8 + pos]
            remote(src, dst_ref, pool_send.at[li], pool_recv.at[li], (base + j) * 2 + core, z).start()

    own = kall.at[pl.ds(TOK, TOK)]
    near_p = remote(
        own, kall.at[pl.ds(pl.multiple_of(core * 512, 256), TOK)],
        near_send.at[0], near_recv.at[0], partner, z,
    )
    near_o = remote(
        own, kall.at[pl.ds(pl.multiple_of((1 - core) * 512, 256), TOK)],
        near_send.at[1], near_recv.at[1], other, z,
    )
    near_p.start()
    near_o.start()

    qb = lax.div(iota((128, TOK), 1), 128) + 2 * d
    r = iota((128, TOK), 0)
    kb = 2 * partner + (r >> 6)
    cbias[0:128] = jnp.where(jnp.abs(kb - qb) > 2, 1.0, NEG_BIG)
    for li in range(4):
        c, n, base, pos = level_peers(li)
        rr = r & 63
        chips = base + (rr >> (6 - li))
        first = (chips * 2 + (r >> 6)) * TOK + (rr & (n - 1)) * (4 << li)
        cbias[128 * (li + 1) : 128 * (li + 2)] = jnp.where(
            jnp.abs((first >> 7) - qb) > 2, float(li + 2), NEG_BIG
        )
    loads[3].wait()
    gain = gain_ref[...]
    back[...] = (cotv[...].astype(F32) * gain).T
    loads[2].wait()

    def half_ref(li, which):
        if li < 3:
            row = pl.multiple_of(NEAR + 128 * (li + 1) + which * 64, 64)
            return kall.at[pl.ds(row, 64)]
        return buf5.at[pl.ds(which * 8, 8)]

    fwds = []
    for li in range(4):
        mine = half_ref(li, core)
        wait_bytes(mine, pool_recv.at[li])
        fwd = remote(mine, mine, fwd_send.at[li], fwd_recv.at[li], partner, z)
        fwd.start()
        fwds.append(fwd)

    near_p.wait_recv()
    p1 = pool_matrix(128, 1).astype(BF16)
    part = kall[pl.ds(pl.multiple_of((1 - core) * 512, 256), TOK), :]
    kall[NEAR : NEAR + 128, :] = dot(p1, part, 1, 0).astype(BF16)

    for li in range(4):
        fwds[li].wait_recv()
    five = buf5[...].astype(F32)
    kall[ROWS - 128 : ROWS, 0:256] = five[:, 0:8, :].reshape(128, 256).astype(BF16)
    kall[ROWS - 128 : ROWS, 256:512] = five[:, 8:16, :].reshape(128, 256).astype(BF16)

    def kcols(h):
        return slice(h * HS, (h + 1) * HS)

    def vcols(h):
        return slice(256 + h * HS, 256 + (h + 1) * HS)

    def group(h, lo, hi, bias):
        s = dot(kall[lo:hi, kcols(h)], qv[:, kcols(h)], 1, 1) * (SCALE * LOG2E) + bias
        top = jnp.max(s, axis=0, keepdims=True)
        p = jnp.exp2(s - top)
        total = jnp.sum(p, axis=0, keepdims=True)
        pt[h, lo:hi, :] = p.astype(BF16)
        out = dot(kall[lo:hi, vcols(h)], pt[h, lo:hi, :], 0, 0)
        return top, total, out

    coarse = [group(h, NEAR, ROWS, cbias[...]) for h in range(2)]

    near_o.wait_recv()
    lane_block = lax.div(iota((1, TOK), 1), 128)
    rows_bias = []
    for e in range(6):
        vals = []
        for i in range(2):
            if e - i < 0 or e - i > 4:
                vals.append(NEG_BIG)
                continue
            want = 2 * d - 2 + e
            hit = jnp.int32(0)
            for j in range(SLOTS):
                ok = jnp.where(nb_ref[i, j] == want, 1, 0) * jnp.where(nc_ref[i] > j, 1, 0)
                hit = jnp.maximum(hit, ok)
            vals.append(jnp.where(hit > 0, 0.0, NEG_BIG))
        row = jnp.where(lane_block == 0, vals[0], vals[1])
        rows_bias.append(jnp.broadcast_to(row, (128, TOK)))
    nbias = jnp.concatenate(rows_bias, axis=0)
    near = [group(h, 0, NEAR, nbias) for h in range(2)]

    attn, alphas, scaled = [], [], []
    usum = jnp.zeros((1, TOK), F32)
    vsum = jnp.zeros((1, TOK), F32)
    for h in range(2):
        m1, t1, o1 = near[h]
        m2, t2, o2 = coarse[h]
        top = jnp.maximum(m1, m2)
        a1 = jnp.exp2(m1 - top)
        a2 = jnp.exp2(m2 - top)
        inv_total = 1.0 / (a1 * t1 + a2 * t2)
        a1 = a1 * inv_total
        a2 = a2 * inv_total
        out = o1 * a1 + o2 * a2
        sc = out * hs_ref[h]
        usum = usum + jnp.sum(sc * sc, axis=0, keepdims=True)
        vsum = vsum + jnp.sum(sc * back[kcols(h), :], axis=0, keepdims=True)
        attn.append(out)
        alphas.append((a1, a2))
        scaled.append(sc)
    ps_own[0:1, :] = usum
    ps_own[1:2, :] = vsum
    for m in range(1, n_head):
        remote(
            ps_own, ps_buf.at[m - 1], ps_sem.at[0], ps_sem.at[1], d, lax.rem(z + m, n_head)
        ).start()

    u = iota((TOK, TOK), 0)
    col = iota((TOK, TOK), 1)
    lvl = (col >> 6) + 2
    rel = (col & 63) & ((256 >> lvl) - 1)
    spread = jnp.where(
        (u >> lvl) == rel,
        jnp.where(lvl == 2, 0.25, jnp.where(lvl == 3, 0.125, jnp.where(lvl == 4, 0.0625, 0.03125))),
        0.0,
    ).astype(BF16)
    e1 = jnp.where(
        (iota((TOK, 128), 0) >> 1) == iota((TOK, 128), 1), 0.5, 0.0
    ).astype(BF16)

    wait_bytes(ps_buf, ps_sem.at[1])
    sums = ps_own[...] + jnp.sum(ps_buf[...], axis=0)
    inv = lax.rsqrt(sums[0:1, :] / width + NORM_EPS)
    fac = inv * inv * (sums[1:2, :] / width)

    d_group = []
    for h in range(2):
        d_attn = (inv * hs_ref[h]) * (back[kcols(h), :] - scaled[h] * fac)
        d_group.append([(d_attn * a).astype(BF16) for a in alphas[h]])

    def backward(h, g, lo, hi, keep, off):
        dg = d_group[h][g]
        delta = jnp.sum(dg.astype(F32) * attn[h], axis=0, keepdims=True)
        dp = dot(kall[lo:hi, vcols(h)], dg, 1, 0)
        pg = pt[h, lo:hi, :]
        ds = (pg.astype(F32) * (dp - delta)).astype(BF16)
        dst[h, lo:hi, :] = ds
        keep[:, kcols(h)] = dot(ds, qv[:, kcols(h)], 1, 0) * SCALE
        keep[:, vcols(h)] = dot(pg, dg, 1, 1)

    for h in range(2):
        backward(h, 1, NEAR, ROWS, cg, NEAR)
    for li in range(4):
        row = pl.multiple_of(128 * (li + 1) + (1 - core) * 64, 64)
        c_send[64 * li : 64 * (li + 1), :] = cg[pl.ds(row, 64), :].astype(BF16)
    swap = remote(c_send, c_recv, cp_sem.at[0], cp_sem.at[1], partner, z)
    swap.start()

    for h in range(2):
        backward(h, 0, 0, NEAR, ext, 0)
    rim_out[1] = ext[pl.ds(pl.multiple_of(core * 512, 256), TOK), :].astype(BF16)
    rim_o = remote(rim_out.at[1], rim_in.at[1], rim_send.at[1], rim_recv.at[1], other, z)
    rim_o.start()
    rim_out[0] = (
        ext[pl.ds(pl.multiple_of((1 - core) * 512, 256), TOK), :]
        + dot(e1, cg[0:128, :].astype(BF16), 1, 0)
    ).astype(BF16)
    rim_p = remote(rim_out.at[0], rim_in.at[0], rim_send.at[0], rim_recv.at[0], partner, z)
    rim_p.start()

    swap.wait_recv()
    for li in range(4):
        row = pl.multiple_of(128 * (li + 1) + core * 64, 64)
        total = cg[pl.ds(row, 64), :] + c_recv[64 * li : 64 * (li + 1), :].astype(F32)
        if li < 3:
            csum[64 * li : 64 * (li + 1), :] = total.astype(BF16)
        else:
            csum5[...] = jnp.concatenate(
                [total[:, 0:256].reshape(8, 8, 256), total[:, 256:512].reshape(8, 8, 256)], axis=1
            ).astype(BF16)
        c, n, base, pos = level_peers(li)
        for j in range(c):
            if li < 3:
                src = csum.at[pl.ds(64 * li + j * n, n)]
                dst_ref = ret.at[pl.ds(pl.multiple_of(64 * li + pos * n, 16), n)]
            else:
                src = csum5.at[j]
                dst_ref = ret5.at[pos]
            remote(src, dst_ref, ret_send.at[li], ret_recv.at[li], (base + j) * 2 + core, z).start()

    for h in range(2):
        mixed_v[:, kcols(h)] = ((scaled[h] * inv).T * gain[:, kcols(h)]).astype(BF16)
    out_m = pltpu.make_async_copy(mixed_v, mixed_hbm, out_sem.at[0])
    out_m.start()
    for h in range(2):
        gqt = dot(kall[:, kcols(h)], dst[h], 0, 0) * SCALE
        gq_v[:, kcols(h)] = gqt.T.astype(BF16)
    out_q = pltpu.make_async_copy(gq_v, gq_hbm, out_sem.at[1])
    out_q.start()

    rim_p.wait_recv()
    rim_o.wait_recv()
    grad = ext[TOK : 2 * TOK, :] + rim_in[0].astype(F32) + rim_in[1].astype(F32)
    for li in range(3):
        wait_bytes(ret.at[pl.ds(64 * li, 64)], ret_recv.at[li])
    wait_bytes(ret5, ret_recv.at[3])
    last = ret5[...].astype(F32)
    last = jnp.concatenate(
        [last[:, 0:8, :].reshape(64, 256), last[:, 8:16, :].reshape(64, 256)], axis=1
    ).astype(BF16)
    whole = jnp.concatenate([ret[...], last], axis=0)
    grad = grad + dot(spread, whole, 1, 0)
    gk_v[...] = grad[:, 0:256].astype(BF16)
    out_k = pltpu.make_async_copy(gk_v, gk_hbm, out_sem.at[2])
    out_k.start()
    gv_v[...] = grad[:, 256:512].astype(BF16)
    out_v = pltpu.make_async_copy(gv_v, gv_hbm, out_sem.at[3])
    out_v.start()

    for li in range(4):
        shape = ret.at[pl.ds(64 * min(li, 2), 64)] if li < 3 else ret5
        wait_bytes(shape, pool_send.at[li])
        wait_bytes(shape, ret_send.at[li])
        fwds[li].wait_send()
    near_p.wait_send()
    near_o.wait_send()
    wait_bytes(ps_buf, ps_sem.at[0])
    swap.wait_send()
    rim_p.wait_send()
    rim_o.wait_send()
    out_m.wait()
    out_q.wait()
    out_k.wait()
    out_v.wait()


def solution(mesh):
    n_ctx, n_head = mesh.shape["ctx"], mesh.shape["head"]
    anywhere = pl.BlockSpec(memory_space=pl.ANY)
    smem = pl.BlockSpec(memory_space=pltpu.SMEM)
    vmem = pl.BlockSpec(memory_space=pltpu.VMEM)
    dma = pltpu.SemaphoreType.DMA

    def body(queries, keys, values, near_blocks, near_count, head_scale, gain, cotangent):
        out = jax.ShapeDtypeStruct((TOK, 256), BF16)
        return pl.pallas_call(
            functools.partial(kernel, n_ctx, n_head),
            out_shape=(out, out, out, out),
            in_specs=[anywhere, anywhere, anywhere, smem, smem, smem, vmem, anywhere],
            out_specs=(anywhere, anywhere, anywhere, anywhere),
            scratch_shapes=[
                pltpu.VMEM((ROWS, COLS), BF16),
                pltpu.VMEM((TOK, 256), BF16),
                pltpu.VMEM((TOK, 256), BF16),
                pltpu.VMEM((112, COLS), BF16),
                pltpu.VMEM((16, 256), BF16),
                pltpu.VMEM((16, 16, 256), BF16),
                pltpu.VMEM((2, TOK), F32),
                pltpu.VMEM((n_head - 1, 2, TOK), F32),
                pltpu.VMEM((COARSE, TOK), F32),
                pltpu.VMEM((256, TOK), F32),
                pltpu.VMEM((2, ROWS, TOK), BF16),
                pltpu.VMEM((2, ROWS, TOK), BF16),
                pltpu.VMEM((COARSE, COLS), F32),
                pltpu.VMEM((NEAR, COLS), F32),
                pltpu.VMEM((256, COLS), BF16),
                pltpu.VMEM((256, COLS), BF16),
                pltpu.VMEM((2, TOK, COLS), BF16),
                pltpu.VMEM((2, TOK, COLS), BF16),
                pltpu.VMEM((192, COLS), BF16),
                pltpu.VMEM((8, 16, 256), BF16),
                pltpu.VMEM((192, COLS), BF16),
                pltpu.VMEM((8, 16, 256), BF16),
                pltpu.VMEM((TOK, 256), BF16),
                pltpu.VMEM((TOK, 256), BF16),
                pltpu.VMEM((TOK, 256), BF16),
                pltpu.VMEM((TOK, 256), BF16),
                dma((4,)), dma((4,)), dma((4,)), dma((4,)), dma((4,)), dma((4,)),
                dma((2,)), dma((2,)), dma((2,)), dma((2,)), dma((2,)), dma((2,)),
                dma((4,)), dma((4,)),
            ],
            compiler_params=pltpu.CompilerParams(
                collective_id=0, has_side_effects=True, vmem_limit_bytes=40 * 1024 * 1024
            ),
        )(queries, keys, values, near_blocks, near_count, head_scale, gain.reshape(1, 256), cotangent)

    return jax.shard_map(
        body,
        mesh=mesh,
        in_specs=(
            P("ctx", "head"), P("ctx", "head"), P("ctx", "head"), P("ctx", None),
            P("ctx"), P("head"), P("head"), P("ctx", "head"),
        ),
        out_specs=(P("ctx", "head"), P("ctx", "head"), P("ctx", "head"), P("ctx", "head")),
        check_vma=False,
    )
```

time: 261 us -> 55.9 us (0.21)
  waiting for transfers between devices: 65.4 us -> 0 us
  matrix products: 55.1 us -> 0 us
  Pallas kernels: 0 us -> 46.8 us
  starting transfers between devices: 41.8 us -> 0 us
  blocking collectives: 25.6 us -> 0 us
  other arithmetic: 24.1 us -> 0 us
  local copies, waits for them, and re-layouts: 30.9 us -> 8.25 us
  between operations: 16.8 us -> 0.67 us
    all_gather x1 -> x0, waiting for transfers between devices: 56.8 us -> none  [body(): lax.all_gather(packed, 'ctx', axis=0, tiled=True)]
    dot_general x74 -> x0, matrix products: 55.1 us -> none  [the longest x10 12.6 us: body(): jnp.dot(ds_far, coarse_k[level_idx], preferred_element_type=jnp.float32)]
    pallas_call x0 -> x1, Pallas kernels: none -> 46.8 us  [body(): pl.pallas_call(functools.partial(kernel, n_ctx, n_head), out_shape=(out,...]
    ppermute x9 -> x0, starting transfers between devices: 41.8 us -> none  [the longest x5 20.5 us: from_partner(): return lax.ppermute(value, axis, pairs)]
    psum x1 -> x0, blocking collectives: 25.6 us -> none  [body(): squares = lax.psum(jnp.sum(scaled * scaled, axis=1), 'head')]
    slice x11 -> x0, local copies, waits for them, and re-layouts: 12.2 us -> none  [the longest x4 6.85 us: body(): piece = everyone[:, offset:offset + count_rows]]
    ppermute x9 -> x0, waiting for transfers between devices: 8.54 us -> none  [the longest x5 8.53 us: from_partner(): return lax.ppermute(value, axis, pairs)]
    reshape x7 -> x0, local copies, waits for them, and re-layouts: 7.42 us -> none  [the longest x2 3.32 us: body(): attention_output = jnp.einsum('itp,ipc->itc', near_weight_rows, near_valu...]
  transfers between devices with their start and end apart: 10 -> 0, of which waited for: 3 -> 0; matrix products, arithmetic and copies ran while one was open for 17% -> 0% of each run, Pallas kernels for 0% -> 0%
where the time goes in v1:
time: 55.9 us; the launch traced here: 55.7 us
  Pallas kernels  46.8 us (84%)
  local copies, waits for them, and re-layouts  8.25 us (15%)
  between operations  0.67 us (1%)
    pallas_call x1, Pallas kernels, body(): pl.pallas_call(functools.partial(kernel, n_ctx, n_head), out_shape=(out,...  46.8 us
    unnamed x20, local copies, waits for them, and re-layouts  8.25 us

profile of v1, /device:TPU:1, one launch (start us, length us, event | category | flops | bytes accessed | tf_op | source)
XLA Modules:
  0.0 55.7 jit_solution(3469177744454079852)
XLA Ops:
  0.6 0.0 copy-start.6
  0.6 0.0 copy-start.4
  0.7 0.6 %copy-done.6 = s32[2]{0:T(128)S(1)} copy-done((s32[2]{0:T(128)S(1)}, s32[2]{0:T(128)}, u32[]{:S(2)}) %copy-start.6) | copy-done | bytes 32
  1.3 0.0 copy-done.4
  1.3 0.0 copy-start
  1.3 0.9 %copy-done = bf16[256,256]{1,0:T(8,128)(2,1)S(1)} copy-done((bf16[256,256]{1,0:T(8,128)(2,1)S(1)}, bf16[256,256]{1,0:T(8,128)(2,1)}, u32[]{:S(2)}) %copy-start) | copy-done | bytes 131096
  2.2 0.0 copy-start.1
  2.2 0.9 %copy-done.1 = bf16[256,256]{1,0:T(8,128)(2,1)S(1)} copy-done((bf16[256,256]{1,0:T(8,128)(2,1)S(1)}, bf16[256,256]{1,0:T(8,128)(2,1)}, u32[]{:S(2)}) %copy-start.1) | copy-done | bytes 131096
  3.1 0.0 copy-start.2
  3.1 0.9 %copy-done.2 = bf16[256,256]{1,0:T(8,128)(2,1)S(1)} copy-done((bf16[256,256]{1,0:T(8,128)(2,1)S(1)}, bf16[256,256]{1,0:T(8,128)(2,1)}, u32[]{:S(2)}) %copy-start.2) | copy-done | bytes 131096
  4.0 0.0 copy-start.3
  4.0 0.9 %copy-done.3 = bf16[256,256]{1,0:T(8,128)(2,1)S(1)} copy-done((bf16[256,256]{1,0:T(8,128)(2,1)S(1)}, bf16[256,256]{1,0:T(8,128)(2,1)}, u32[]{:S(2)}) %copy-start.3) | copy-done | bytes 131096
  4.9 0.0 copy-start.5
  5.0 0.7 %copy-done.5 = f32[256]{0:T(256)S(1)} copy-done((f32[256]{0:T(256)S(1)}, f32[256]{0:T(256)}, u32[]{:S(2)}) %copy-start.5) | copy-done | bytes 1048
  5.6 0.0 copy-start.7
  5.6 0.7 %copy-done.7 = f32[2]{0:T(128)S(1)} copy-done((f32[2]{0:T(128)S(1)}, f32[2]{0:T(128)}, u32[]{:S(2)}) %copy-start.7) | copy-done | bytes 32
  6.3 46.8 %shard_map.111 = (bf16[256,256]{1,0:T(8,128)(2,1)S(1)}, bf16[256,256]{1,0:T(8,128)(2,1)S(1)}, bf16[256,256]{1,0:T(8,128)(2,1)S(1)}, bf16[256,256]{1,0:T(8,128)(2,1)S(1)}) custom-call(bf16[256,256]{1,0:T(8,128)(2,1)S(1)} %copy-done, bf16[256,256]{1,0:T(8,128)(2,1)S(1)} %copy-done.1, bf16[256,256]{1,0:T(8,128)(2,1)S(1)} %copy-done.2, s32[2,4]{1,0:T(2,128)S(1)} %copy-done.4, ...), custom_call_target="tpu_custom_call" | custom-call | tf_op jit(solution)/shard_map/pallas_call | solution.py:369
  53.1 0.7 %copy.16 = bf16[256,256]{1,0:T(8,128)(2,1)} copy(bf16[256,256]{1,0:T(8,128)(2,1)S(1)} %get-tuple-element.8) | data formatting | bytes 262144
  53.7 0.7 %copy.17 = bf16[256,256]{1,0:T(8,128)(2,1)} copy(bf16[256,256]{1,0:T(8,128)(2,1)S(1)} %get-tuple-element.9) | data formatting | bytes 262144
  54.4 0.7 %copy.18 = bf16[256,256]{1,0:T(8,128)(2,1)} copy(bf16[256,256]{1,0:T(8,128)(2,1)S(1)} %get-tuple-element.10) | data formatting | bytes 262144
  55.1 0.7 %copy.19 = bf16[256,256]{1,0:T(8,128)(2,1)} copy(bf16[256,256]{1,0:T(8,128)(2,1)S(1)} %get-tuple-element.11) | data formatting | bytes 262144
Async XLA Ops:
  0.6 0.7 %copy-start.6 = (s32[2]{0:T(128)S(1)}, s32[2]{0:T(128)}, u32[]{:S(2)}) copy-start(s32[2]{0:T(128)} %nc_ref.1) | copy-start | bytes 28
  0.6 0.7 %copy-start.4 = (s32[2,4]{1,0:T(2,128)S(1)}, s32[2,4]{1,0:T(2,128)}, u32[]{:S(2)}) copy-start(s32[2,4]{1,0:T(2,128)} %nb_ref.1) | copy-start | bytes 100
  1.3 0.9 %copy-start = (bf16[256,256]{1,0:T(8,128)(2,1)S(1)}, bf16[256,256]{1,0:T(8,128)(2,1)}, u32[]{:S(2)}) copy-start(bf16[256,256]{1,0:T(8,128)(2,1)} %q_hbm.1) | copy-start | bytes 393220
  2.2 0.9 %copy-start.1 = (bf16[256,256]{1,0:T(8,128)(2,1)S(1)}, bf16[256,256]{1,0:T(8,128)(2,1)}, u32[]{:S(2)}) copy-start(bf16[256,256]{1,0:T(8,128)(2,1)} %k_hbm.1) | copy-start | bytes 393220
  3.1 0.9 %copy-start.2 = (bf16[256,256]{1,0:T(8,128)(2,1)S(1)}, bf16[256,256]{1,0:T(8,128)(2,1)}, u32[]{:S(2)}) copy-start(bf16[256,256]{1,0:T(8,128)(2,1)} %v_hbm.1) | copy-start | bytes 393220
  4.0 0.9 %copy-start.3 = (bf16[256,256]{1,0:T(8,128)(2,1)S(1)}, bf16[256,256]{1,0:T(8,128)(2,1)}, u32[]{:S(2)}) copy-start(bf16[256,256]{1,0:T(8,128)(2,1)} %cot_hbm.1) | copy-start | bytes 393220
  4.9 0.7 %copy-start.5 = (f32[256]{0:T(256)S(1)}, f32[256]{0:T(256)}, u32[]{:S(2)}) copy-start(f32[256]{0:T(256)} %param.14) | copy-start | bytes 3076
  5.6 0.7 %copy-start.7 = (f32[2]{0:T(128)S(1)}, f32[2]{0:T(128)}, u32[]{:S(2)}) copy-start(f32[2]{0:T(128)} %hs_ref.1) | copy-start | bytes 28

commit v2 on v1

--- a/solution.py
+++ b/solution.py
@@ -41,12 +41,12 @@
 
 def kernel(
     n_ctx, n_head,
-    q_hbm, k_hbm, v_hbm, nb_ref, nc_ref, hs_ref, gain_ref, cot_hbm,
-    mixed_hbm, gq_hbm, gk_hbm, gv_hbm,
+    q_hbm, k_hbm, v_hbm, nb_hbm, nc_hbm, hs_hbm, gain_hbm, cot_hbm,
+    mixed_v, gq_v, gk_v, gv_v,
+    nb_ref, nc_ref, hs_ref, gain_v,
     kall, qv, cotv, pool, pool5, buf5, ps_own, ps_buf, cbias, back,
     pt, dst, cg, ext, c_send, c_recv, rim_out, rim_in, csum, csum5, ret, ret5,
-    mixed_v, gq_v, gk_v, gv_v,
-    ld_sem, out_sem, pool_send, pool_recv, fwd_send, fwd_recv, near_send, near_recv,
+    ld_sem, pool_send, pool_recv, fwd_send, fwd_recv, near_send, near_recv,
     ps_sem, cp_sem, rim_send, rim_recv, ret_send, ret_recv,
 ):
     d = lax.axis_index("ctx")
@@ -86,6 +86,10 @@
         pltpu.make_async_copy(v_hbm, kall.at[pl.ds(TOK, TOK), pl.ds(256, 256)], ld_sem.at[1]),
         pltpu.make_async_copy(q_hbm, qv, ld_sem.at[2]),
         pltpu.make_async_copy(cot_hbm, cotv, ld_sem.at[3]),
+        pltpu.make_async_copy(gain_hbm, gain_v, ld_sem.at[4]),
+        pltpu.make_async_copy(nb_hbm, nb_ref, ld_sem.at[5]),
+        pltpu.make_async_copy(nc_hbm, nc_ref, ld_sem.at[6]),
+        pltpu.make_async_copy(hs_hbm, hs_ref, ld_sem.at[7]),
     ]
     for load in loads:
         load.start()
@@ -146,8 +150,11 @@
             jnp.abs((first >> 7) - qb) > 2, float(li + 2), NEG_BIG
         )
     loads[3].wait()
-    gain = gain_ref[...]
+    loads[4].wait()
+    gain = gain_v[...].reshape(1, 256)
     back[...] = (cotv[...].astype(F32) * gain).T
+    for load in loads[5:]:
+        load.wait()
     loads[2].wait()
 
     def half_ref(li, which):
@@ -313,13 +320,9 @@
 
     for h in range(2):
         mixed_v[:, kcols(h)] = ((scaled[h] * inv).T * gain[:, kcols(h)]).astype(BF16)
-    out_m = pltpu.make_async_copy(mixed_v, mixed_hbm, out_sem.at[0])
-    out_m.start()
     for h in range(2):
         gqt = dot(kall[:, kcols(h)], dst[h], 0, 0) * SCALE
         gq_v[:, kcols(h)] = gqt.T.astype(BF16)
-    out_q = pltpu.make_async_copy(gq_v, gq_hbm, out_sem.at[1])
-    out_q.start()
 
     rim_p.wait_recv()
     rim_o.wait_recv()
@@ -334,11 +337,7 @@
     whole = jnp.concatenate([ret[...], last], axis=0)
     grad = grad + dot(spread, whole, 1, 0)
     gk_v[...] = grad[:, 0:256].astype(BF16)
-    out_k = pltpu.make_async_copy(gk_v, gk_hbm, out_sem.at[2])
-    out_k.start()
     gv_v[...] = grad[:, 256:512].astype(BF16)
-    out_v = pltpu.make_async_copy(gv_v, gv_hbm, out_sem.at[3])
-    out_v.start()
 
     for li in range(4):
         shape = ret.at[pl.ds(64 * min(li, 2), 64)] if li < 3 else ret5
@@ -351,27 +350,26 @@
     swap.wait_send()
     rim_p.wait_send()
     rim_o.wait_send()
-    out_m.wait()
-    out_q.wait()
-    out_k.wait()
-    out_v.wait()
 
 
 def solution(mesh):
     n_ctx, n_head = mesh.shape["ctx"], mesh.shape["head"]
-    anywhere = pl.BlockSpec(memory_space=pl.ANY)
-    smem = pl.BlockSpec(memory_space=pltpu.SMEM)
+    hbm = pl.BlockSpec(memory_space=pl.ANY)
     vmem = pl.BlockSpec(memory_space=pltpu.VMEM)
     dma = pltpu.SemaphoreType.DMA
 
     def body(queries, keys, values, near_blocks, near_count, head_scale, gain, cotangent):
         out = jax.ShapeDtypeStruct((TOK, 256), BF16)
-        return pl.pallas_call(
+        outs = pl.pallas_call(
             functools.partial(kernel, n_ctx, n_head),
             out_shape=(out, out, out, out),
-            in_specs=[anywhere, anywhere, anywhere, smem, smem, smem, vmem, anywhere],
-            out_specs=(anywhere, anywhere, anywhere, anywhere),
+            in_specs=[hbm] * 8,
+            out_specs=(vmem, vmem, vmem, vmem),
             scratch_shapes=[
+                pltpu.SMEM((2, SLOTS), jnp.int32),
+                pltpu.SMEM((2,), jnp.int32),
+                pltpu.SMEM((2,), F32),
+                pltpu.VMEM((256,), F32),
                 pltpu.VMEM((ROWS, COLS), BF16),
                 pltpu.VMEM((TOK, 256), BF16),
                 pltpu.VMEM((TOK, 256), BF16),
@@ -394,18 +392,15 @@
                 pltpu.VMEM((8, 16, 256), BF16),
                 pltpu.VMEM((192, COLS), BF16),
                 pltpu.VMEM((8, 16, 256), BF16),
-                pltpu.VMEM((TOK, 256), BF16),
-                pltpu.VMEM((TOK, 256), BF16),
-                pltpu.VMEM((TOK, 256), BF16),
-                pltpu.VMEM((TOK, 256), BF16),
-                dma((4,)), dma((4,)), dma((4,)), dma((4,)), dma((4,)), dma((4,)),
+                dma((8,)), dma((4,)), dma((4,)), dma((4,)), dma((4,)),
                 dma((2,)), dma((2,)), dma((2,)), dma((2,)), dma((2,)), dma((2,)),
                 dma((4,)), dma((4,)),
             ],
             compiler_params=pltpu.CompilerParams(
                 collective_id=0, has_side_effects=True, vmem_limit_bytes=40 * 1024 * 1024
             ),
-        )(queries, keys, values, near_blocks, near_count, head_scale, gain.reshape(1, 256), cotangent)
+        )(queries, keys, values, near_blocks, near_count, head_scale, gain, cotangent)
+        return outs
 
     return jax.shard_map(
         body,

time: 55.9 us -> 55.6 us (level)
  Pallas kernels: 46.8 us -> 45.8 us
  local copies, waits for them, and re-layouts: 8.25 us -> 8.9 us
    pallas_call x1, Pallas kernels: 46.8 us -> 45.8 us  [body(): pl.pallas_call(functools.partial(kernel, n_ctx, n_head), out_shape=(out,...]
    unnamed x20, local copies, waits for them, and re-layouts: 8.25 us -> 8.9 us
where the time goes in v2:
time: 55.6 us; the launch traced here: 55.4 us
  Pallas kernels  45.8 us (82%)
  local copies, waits for them, and re-layouts  8.9 us (16%)
  between operations  0.66 us (1%)
    pallas_call x1, Pallas kernels, body(): pl.pallas_call(functools.partial(kernel, n_ctx, n_head), out_shape=(out,...  45.8 us
    unnamed x20, local copies, waits for them, and re-layouts  8.9 us

profile of v2, /device:TPU:1, one launch (start us, length us, event | category | flops | bytes accessed | tf_op | source)
XLA Modules:
  0.0 55.4 jit_solution(4174511414224935188)
XLA Ops:
  0.6 0.0 copy-start
  0.6 0.9 %copy-done = bf16[256,256]{1,0:T(8,128)(2,1)S(1)} copy-done((bf16[256,256]{1,0:T(8,128)(2,1)S(1)}, bf16[256,256]{1,0:T(8,128)(2,1)}, u32[]{:S(2)}) %copy-start) | copy-done | bytes 131096
  1.5 0.0 copy-start.1
  1.5 0.9 %copy-done.1 = bf16[256,256]{1,0:T(8,128)(2,1)S(1)} copy-done((bf16[256,256]{1,0:T(8,128)(2,1)S(1)}, bf16[256,256]{1,0:T(8,128)(2,1)}, u32[]{:S(2)}) %copy-start.1) | copy-done | bytes 131096
  2.4 0.0 copy-start.2
  2.4 0.9 %copy-done.2 = bf16[256,256]{1,0:T(8,128)(2,1)S(1)} copy-done((bf16[256,256]{1,0:T(8,128)(2,1)S(1)}, bf16[256,256]{1,0:T(8,128)(2,1)}, u32[]{:S(2)}) %copy-start.2) | copy-done | bytes 131096
  3.3 0.0 copy-start.3
  3.4 0.9 %copy-done.3 = bf16[256,256]{1,0:T(8,128)(2,1)S(1)} copy-done((bf16[256,256]{1,0:T(8,128)(2,1)S(1)}, bf16[256,256]{1,0:T(8,128)(2,1)}, u32[]{:S(2)}) %copy-start.3) | copy-done | bytes 131096
  4.3 0.0 copy-start.4
  4.3 0.7 %copy-done.4 = s32[2,4]{1,0:T(2,128)S(1)} copy-done((s32[2,4]{1,0:T(2,128)S(1)}, s32[2,4]{1,0:T(2,128)}, u32[]{:S(2)}) %copy-start.4) | copy-done | bytes 56
  4.9 0.0 copy-start.5
  4.9 0.7 %copy-done.5 = f32[256]{0:T(256)S(1)} copy-done((f32[256]{0:T(256)S(1)}, f32[256]{0:T(256)}, u32[]{:S(2)}) %copy-start.5) | copy-done | bytes 1048
  5.6 0.0 copy-start.6
  5.6 0.7 %copy-done.6 = s32[2]{0:T(128)S(1)} copy-done((s32[2]{0:T(128)S(1)}, s32[2]{0:T(128)}, u32[]{:S(2)}) %copy-start.6) | copy-done | bytes 32
  6.3 0.0 copy-start.7
  6.3 0.7 %copy-done.7 = f32[2]{0:T(128)S(1)} copy-done((f32[2]{0:T(128)S(1)}, f32[2]{0:T(128)}, u32[]{:S(2)}) %copy-start.7) | copy-done | bytes 32
  6.9 45.8 %shard_map.111 = (bf16[256,256]{1,0:T(8,128)(2,1)S(1)}, bf16[256,256]{1,0:T(8,128)(2,1)S(1)}, bf16[256,256]{1,0:T(8,128)(2,1)S(1)}, bf16[256,256]{1,0:T(8,128)(2,1)S(1)}) custom-call(bf16[256,256]{1,0:T(8,128)(2,1)S(1)} %copy-done, bf16[256,256]{1,0:T(8,128)(2,1)S(1)} %copy-done.1, bf16[256,256]{1,0:T(8,128)(2,1)S(1)} %copy-done.2, s32[2,4]{1,0:T(2,128)S(1)} %copy-done.4, ...), custom_call_target="tpu_custom_call" | custom-call | tf_op jit(solution)/shard_map/pallas_call | solution.py:363
  52.7 0.7 %copy.16 = bf16[256,256]{1,0:T(8,128)(2,1)} copy(bf16[256,256]{1,0:T(8,128)(2,1)S(1)} %get-tuple-element.8) | data formatting | bytes 262144
  53.4 0.7 %copy.17 = bf16[256,256]{1,0:T(8,128)(2,1)} copy(bf16[256,256]{1,0:T(8,128)(2,1)S(1)} %get-tuple-element.9) | data formatting | bytes 262144
  54.1 0.7 %copy.18 = bf16[256,256]{1,0:T(8,128)(2,1)} copy(bf16[256,256]{1,0:T(8,128)(2,1)S(1)} %get-tuple-element.10) | data formatting | bytes 262144
  54.7 0.7 %copy.19 = bf16[256,256]{1,0:T(8,128)(2,1)} copy(bf16[256,256]{1,0:T(8,128)(2,1)S(1)} %get-tuple-element.11) | data formatting | bytes 262144
Async XLA Ops:
  0.6 0.9 %copy-start = (bf16[256,256]{1,0:T(8,128)(2,1)S(1)}, bf16[256,256]{1,0:T(8,128)(2,1)}, u32[]{:S(2)}) copy-start(bf16[256,256]{1,0:T(8,128)(2,1)} %q_hbm.1) | copy-start | bytes 393220
  1.5 0.9 %copy-start.1 = (bf16[256,256]{1,0:T(8,128)(2,1)S(1)}, bf16[256,256]{1,0:T(8,128)(2,1)}, u32[]{:S(2)}) copy-start(bf16[256,256]{1,0:T(8,128)(2,1)} %k_hbm.1) | copy-start | bytes 393220
  2.4 0.9 %copy-start.2 = (bf16[256,256]{1,0:T(8,128)(2,1)S(1)}, bf16[256,256]{1,0:T(8,128)(2,1)}, u32[]{:S(2)}) copy-start(bf16[256,256]{1,0:T(8,128)(2,1)} %v_hbm.1) | copy-start | bytes 393220
  3.3 0.9 %copy-start.3 = (bf16[256,256]{1,0:T(8,128)(2,1)S(1)}, bf16[256,256]{1,0:T(8,128)(2,1)}, u32[]{:S(2)}) copy-start(bf16[256,256]{1,0:T(8,128)(2,1)} %cot_hbm.1) | copy-start | bytes 393220
  4.3 0.7 %copy-start.4 = (s32[2,4]{1,0:T(2,128)S(1)}, s32[2,4]{1,0:T(2,128)}, u32[]{:S(2)}) copy-start(s32[2,4]{1,0:T(2,128)} %nb_hbm.1) | copy-start | bytes 100
  4.9 0.7 %copy-start.5 = (f32[256]{0:T(256)S(1)}, f32[256]{0:T(256)}, u32[]{:S(2)}) copy-start(f32[256]{0:T(256)} %gain_hbm.1) | copy-start | bytes 3076
  5.6 0.7 %copy-start.6 = (s32[2]{0:T(128)S(1)}, s32[2]{0:T(128)}, u32[]{:S(2)}) copy-start(s32[2]{0:T(128)} %nc_hbm.1) | copy-start | bytes 28
  6.3 0.7 %copy-start.7 = (f32[2]{0:T(128)S(1)}, f32[2]{0:T(128)}, u32[]{:S(2)}) copy-start(f32[2]{0:T(128)} %hs_hbm.1) | copy-start | bytes 28

commit v3 on v2

--- a/solution.py
+++ b/solution.py
@@ -352,6 +352,17 @@
     rim_o.wait_send()
 
 
+def store(a, b, c, e, a_hbm, b_hbm, c_hbm, e_hbm, sem):
+    copies = [
+        pltpu.make_async_copy(src, dst_ref, sem.at[i])
+        for i, (src, dst_ref) in enumerate(((a, a_hbm), (b, b_hbm), (c, c_hbm), (e, e_hbm)))
+    ]
+    for copy in copies:
+        copy.start()
+    for copy in copies:
+        copy.wait()
+
+
 def solution(mesh):
     n_ctx, n_head = mesh.shape["ctx"], mesh.shape["head"]
     hbm = pl.BlockSpec(memory_space=pl.ANY)
@@ -362,7 +373,7 @@
         out = jax.ShapeDtypeStruct((TOK, 256), BF16)
         outs = pl.pallas_call(
             functools.partial(kernel, n_ctx, n_head),
-            out_shape=(out, out, out, out),
+            out_shape=(pltpu.VMEM((TOK, 256), BF16),) * 4,
             in_specs=[hbm] * 8,
             out_specs=(vmem, vmem, vmem, vmem),
             scratch_shapes=[
@@ -397,10 +408,17 @@
                 dma((4,)), dma((4,)),
             ],
             compiler_params=pltpu.CompilerParams(
-                collective_id=0, has_side_effects=True, vmem_limit_bytes=40 * 1024 * 1024
+                collective_id=0, has_side_effects=True, vmem_limit_bytes=56 * 1024 * 1024
             ),
         )(queries, keys, values, near_blocks, near_count, head_scale, gain, cotangent)
-        return outs
+        return pl.pallas_call(
+            store,
+            out_shape=(out, out, out, out),
+            in_specs=[hbm] * 4,
+            out_specs=(hbm, hbm, hbm, hbm),
+            scratch_shapes=[dma((4,))],
+            compiler_params=pltpu.CompilerParams(vmem_limit_bytes=1024 * 1024),
+        )(*outs)
 
     return jax.shard_map(
         body,

time: 55.6 us -> 47.4 us (0.85)
  local copies, waits for them, and re-layouts: 8.9 us -> 0 us
  Pallas kernels: 45.8 us -> 46.6 us
    unnamed x20 -> x0, local copies, waits for them, and re-layouts: 8.9 us -> none
    pallas_call x1 -> x2, Pallas kernels: 45.8 us -> 46.6 us  [the longest x1 45.8 us: body(): pl.pallas_call(functools.partial(kernel, n_ctx, n_head), out_shape=(pltpu...]
where the time goes in v3:
time: 47.4 us; the launch traced here: 47.3 us
  Pallas kernels  46.6 us (98%)
  between operations  0.64 us (1%)
    pallas_call x1, Pallas kernels, body(): pl.pallas_call(functools.partial(kernel, n_ctx, n_head), out_shape=(pltpu...  45.8 us

profile of v3, /device:TPU:1, one launch (start us, length us, event | category | flops | bytes accessed | tf_op | source)
XLA Modules:
  0.0 47.3 jit_solution(13225584624209462809)
XLA Ops:
  0.6 45.8 %shard_map.111 = (bf16[256,256]{1,0:T(8,128)(2,1)S(1)}, bf16[256,256]{1,0:T(8,128)(2,1)S(1)}, bf16[256,256]{1,0:T(8,128)(2,1)S(1)}, bf16[256,256]{1,0:T(8,128)(2,1)S(1)}) custom-call(bf16[256,256]{1,0:T(8,128)(2,1)} %q_hbm.1, bf16[256,256]{1,0:T(8,128)(2,1)} %k_hbm.1, bf16[256,256]{1,0:T(8,128)(2,1)} %v_hbm.1, s32[2,4]{1,0:T(2,128)} %nb_hbm.1, s32[2]{0:T(128)} %nc_hbm.1, ...), custom_call_target="tpu_custom_call" | custom-call | tf_op jit(solution)/shard_map/pallas_call | solution.py:374
  46.5 0.8 %shard_map.112 = (bf16[256,256]{1,0:T(8,128)(2,1)}, bf16[256,256]{1,0:T(8,128)(2,1)}, bf16[256,256]{1,0:T(8,128)(2,1)}, bf16[256,256]{1,0:T(8,128)(2,1)}) custom-call(bf16[256,256]{1,0:T(8,128)(2,1)S(1)} %get-tuple-element.8.a, bf16[256,256]{1,0:T(8,128)(2,1)S(1)} %get-tuple-element.9.b, bf16[256,256]{1,0:T(8,128)(2,1)S(1)} %get-tuple-element.10.c, ...), custom_call_target="tpu_custom_call" | custom-call | tf_op jit(solution)/shard_map/pallas_call | solution.py:414

commit v4 on v3

--- a/solution.py
+++ b/solution.py
@@ -54,7 +54,8 @@
     n_chip = n_ctx // 2
     chip = lax.div(d, 2)
     core = lax.rem(d, 2)
-    partner = chip * 2 + 1 - core
+    across = 1 - core
+    partner = chip * 2 + across
     other = lax.rem(d + n_ctx - 1 + 2 * core, n_ctx)
     width = float(n_head * 2 * HS)
 
@@ -68,8 +69,7 @@
     for m in range(1, n_head):
         hello(d, lax.rem(z + m, n_head))
     for m in range(1, n_chip):
-        hello(lax.rem(chip + m, n_chip) * 2 + core, z)
-    hello(other, z)
+        hello(lax.rem(chip + m, n_chip) * 2 + across, z)
     hello(partner, z)
 
     def remote(src, dst_ref, ssem, rsem, ctx, head):
@@ -104,7 +104,7 @@
     pool[...] = pooled[0:112].astype(BF16)
     pool5[...] = jnp.concatenate([pooled[112:120, 0:256], pooled[112:120, 256:512]], axis=0).astype(BF16)
 
-    pl.semaphore_wait(barrier, n_head - 1 + n_chip - 1 + 2)
+    pl.semaphore_wait(barrier, n_head - 1 + n_chip - 1 + 1)
 
     def level_peers(li):
         c = 1 << li
@@ -113,7 +113,7 @@
         return c, 64 >> li, base, lax.rem(chip, c)
 
     pool_off = (0, 64, 96)
-    for li in range(4):
+    for li in (3, 2, 1, 0):
         c, n, base, pos = level_peers(li)
         for j in range(c):
             if li < 3:
@@ -123,7 +123,7 @@
             else:
                 src = pool5
                 dst_ref = buf5.at[core * 8 + pos]
-            remote(src, dst_ref, pool_send.at[li], pool_recv.at[li], (base + j) * 2 + core, z).start()
+            remote(src, dst_ref, pool_send.at[li], pool_recv.at[li], (base + j) * 2 + across, z).start()
 
     own = kall.at[pl.ds(TOK, TOK)]
     near_p = remote(
@@ -163,25 +163,6 @@
             return kall.at[pl.ds(row, 64)]
         return buf5.at[pl.ds(which * 8, 8)]
 
-    fwds = []
-    for li in range(4):
-        mine = half_ref(li, core)
-        wait_bytes(mine, pool_recv.at[li])
-        fwd = remote(mine, mine, fwd_send.at[li], fwd_recv.at[li], partner, z)
-        fwd.start()
-        fwds.append(fwd)
-
-    near_p.wait_recv()
-    p1 = pool_matrix(128, 1).astype(BF16)
-    part = kall[pl.ds(pl.multiple_of((1 - core) * 512, 256), TOK), :]
-    kall[NEAR : NEAR + 128, :] = dot(p1, part, 1, 0).astype(BF16)
-
-    for li in range(4):
-        fwds[li].wait_recv()
-    five = buf5[...].astype(F32)
-    kall[ROWS - 128 : ROWS, 0:256] = five[:, 0:8, :].reshape(128, 256).astype(BF16)
-    kall[ROWS - 128 : ROWS, 256:512] = five[:, 8:16, :].reshape(128, 256).astype(BF16)
-
     def kcols(h):
         return slice(h * HS, (h + 1) * HS)
 
@@ -197,9 +178,6 @@
         out = dot(kall[lo:hi, vcols(h)], pt[h, lo:hi, :], 0, 0)
         return top, total, out
 
-    coarse = [group(h, NEAR, ROWS, cbias[...]) for h in range(2)]
-
-    near_o.wait_recv()
     lane_block = lax.div(iota((1, TOK), 1), 128)
     rows_bias = []
     for e in range(6):
@@ -217,6 +195,30 @@
         row = jnp.where(lane_block == 0, vals[0], vals[1])
         rows_bias.append(jnp.broadcast_to(row, (128, TOK)))
     nbias = jnp.concatenate(rows_bias, axis=0)
+    fwds = [None] * 4
+
+    def relay(li):
+        mine = half_ref(li, across)
+        wait_bytes(mine, pool_recv.at[li])
+        fwds[li] = remote(mine, mine, fwd_send.at[li], fwd_recv.at[li], partner, z)
+        fwds[li].start()
+
+    for li in range(4):
+        relay(li)
+    near_p.wait_recv()
+
+    p1 = pool_matrix(128, 1).astype(BF16)
+    part = kall[pl.ds(pl.multiple_of((1 - core) * 512, 256), TOK), :]
+    kall[NEAR : NEAR + 128, :] = dot(p1, part, 1, 0).astype(BF16)
+
+    for li in range(4):
+        fwds[li].wait_recv()
+    five = buf5[...].astype(F32)
+    kall[ROWS - 128 : ROWS, 0:256] = five[:, 0:8, :].reshape(128, 256).astype(BF16)
+    kall[ROWS - 128 : ROWS, 256:512] = five[:, 8:16, :].reshape(128, 256).astype(BF16)
+
+    coarse = [group(h, NEAR, ROWS, cbias[...]) for h in range(2)]
+    near_o.wait_recv()
     near = [group(h, 0, NEAR, nbias) for h in range(2)]
 
     attn, alphas, scaled = [], [], []
@@ -281,7 +283,7 @@
     for h in range(2):
         backward(h, 1, NEAR, ROWS, cg, NEAR)
     for li in range(4):
-        row = pl.multiple_of(128 * (li + 1) + (1 - core) * 64, 64)
+        row = pl.multiple_of(128 * (li + 1) + core * 64, 64)
         c_send[64 * li : 64 * (li + 1), :] = cg[pl.ds(row, 64), :].astype(BF16)
     swap = remote(c_send, c_recv, cp_sem.at[0], cp_sem.at[1], partner, z)
     swap.start()
@@ -299,8 +301,8 @@
     rim_p.start()
 
     swap.wait_recv()
-    for li in range(4):
-        row = pl.multiple_of(128 * (li + 1) + core * 64, 64)
+    for li in (3, 2, 1, 0):
+        row = pl.multiple_of(128 * (li + 1) + across * 64, 64)
         total = cg[pl.ds(row, 64), :] + c_recv[64 * li : 64 * (li + 1), :].astype(F32)
         if li < 3:
             csum[64 * li : 64 * (li + 1), :] = total.astype(BF16)
@@ -316,7 +318,7 @@
             else:
                 src = csum5.at[j]
                 dst_ref = ret5.at[pos]
-            remote(src, dst_ref, ret_send.at[li], ret_recv.at[li], (base + j) * 2 + core, z).start()
+            remote(src, dst_ref, ret_send.at[li], ret_recv.at[li], (base + j) * 2 + across, z).start()
 
     for h in range(2):
         mixed_v[:, kcols(h)] = ((scaled[h] * inv).T * gain[:, kcols(h)]).astype(BF16)

time: 47.4 us -> 45.3 us (0.956)
  Pallas kernels: 46.6 us -> 44.6 us
    pallas_call x1, Pallas kernels: 45.8 us -> 43.7 us  [body(): pl.pallas_call(functools.partial(kernel, n_ctx, n_head), out_shape=(pltpu...]
where the time goes in v4:
time: 45.3 us; the launch traced here: 45.2 us
  Pallas kernels  44.6 us (98%)
  between operations  0.64 us (1%)
    pallas_call x1, Pallas kernels, body(): pl.pallas_call(functools.partial(kernel, n_ctx, n_head), out_shape=(pltpu...  43.7 us

profile of v4, /device:TPU:1, one launch (start us, length us, event | category | flops | bytes accessed | tf_op | source)
XLA Modules:
  0.0 45.2 jit_solution(14889891866330626883)
XLA Ops:
  0.6 43.7 %shard_map.111 = (bf16[256,256]{1,0:T(8,128)(2,1)S(1)}, bf16[256,256]{1,0:T(8,128)(2,1)S(1)}, bf16[256,256]{1,0:T(8,128)(2,1)S(1)}, bf16[256,256]{1,0:T(8,128)(2,1)S(1)}) custom-call(bf16[256,256]{1,0:T(8,128)(2,1)} %q_hbm.1, bf16[256,256]{1,0:T(8,128)(2,1)} %k_hbm.1, bf16[256,256]{1,0:T(8,128)(2,1)} %v_hbm.1, s32[2,4]{1,0:T(2,128)} %nb_hbm.1, s32[2]{0:T(128)} %nc_hbm.1, ...), custom_call_target="tpu_custom_call" | custom-call | tf_op jit(solution)/shard_map/pallas_call | solution.py:376
  44.4 0.8 %shard_map.112 = (bf16[256,256]{1,0:T(8,128)(2,1)}, bf16[256,256]{1,0:T(8,128)(2,1)}, bf16[256,256]{1,0:T(8,128)(2,1)}, bf16[256,256]{1,0:T(8,128)(2,1)}) custom-call(bf16[256,256]{1,0:T(8,128)(2,1)S(1)} %get-tuple-element.8.a, bf16[256,256]{1,0:T(8,128)(2,1)S(1)} %get-tuple-element.9.b, bf16[256,256]{1,0:T(8,128)(2,1)S(1)} %get-tuple-element.10.c, ...), custom_call_target="tpu_custom_call" | custom-call | tf_op jit(solution)/shard_map/pallas_call | solution.py:416

commit v5 on v4

--- a/solution.py
+++ b/solution.py
@@ -45,7 +45,7 @@
     mixed_v, gq_v, gk_v, gv_v,
     nb_ref, nc_ref, hs_ref, gain_v,
     kall, qv, cotv, pool, pool5, buf5, ps_own, ps_buf, cbias, back,
-    pt, dst, cg, ext, c_send, c_recv, rim_out, rim_in, csum, csum5, ret, ret5,
+    pt, dst, cg, ext, c_send, c_recv, rim_out, rim_in, csum, csum5, ret, ret5, ext_o,
     ld_sem, pool_send, pool_recv, fwd_send, fwd_recv, near_send, near_recv,
     ps_sem, cp_sem, rim_send, rim_recv, ret_send, ret_recv,
 ):
@@ -66,12 +66,6 @@
             barrier, inc=1, device_id=(ctx, head), device_id_type=pl.DeviceIdType.MESH
         )
 
-    for m in range(1, n_head):
-        hello(d, lax.rem(z + m, n_head))
-    for m in range(1, n_chip):
-        hello(lax.rem(chip + m, n_chip) * 2 + across, z)
-    hello(partner, z)
-
     def remote(src, dst_ref, ssem, rsem, ctx, head):
         return pltpu.make_async_remote_copy(
             src_ref=src, dst_ref=dst_ref, send_sem=ssem, recv_sem=rsem,
@@ -93,13 +87,18 @@
     ]
     for load in loads:
         load.start()
-    loads[0].wait()
-    loads[1].wait()
+    for m in range(1, n_chip):
+        hello(lax.rem(chip + m, n_chip) * 2 + across, z)
+    hello(partner, z)
+    for m in range(1, n_head):
+        hello(d, lax.rem(z + m, n_head))
 
     pm = jnp.concatenate(
         [pool_matrix(64, 2), pool_matrix(32, 3), pool_matrix(16, 4), pool_matrix(8, 5),
          jnp.zeros((8, TOK), F32)], axis=0,
     ).astype(BF16)
+    loads[0].wait()
+    loads[1].wait()
     pooled = dot(pm, kall[TOK : 2 * TOK, :], 1, 0)
     pool[...] = pooled[0:112].astype(BF16)
     pool5[...] = jnp.concatenate([pooled[112:120, 0:256], pooled[112:120, 256:512]], axis=0).astype(BF16)
@@ -169,32 +168,44 @@
     def vcols(h):
         return slice(256 + h * HS, 256 + (h + 1) * HS)
 
-    def group(h, lo, hi, bias):
-        s = dot(kall[lo:hi, kcols(h)], qv[:, kcols(h)], 1, 1) * (SCALE * LOG2E) + bias
+    local = pl.ds(pl.multiple_of(across * 256, 256), 512)
+    beside = pl.ds(pl.multiple_of(core * 512, 256), 256)
+    far = pl.ds(NEAR, COARSE)
+
+    def group(h, rows, bias):
+        s = dot(kall[rows, kcols(h)], qv[:, kcols(h)], 1, 1) * (SCALE * LOG2E) + bias
         top = jnp.max(s, axis=0, keepdims=True)
         p = jnp.exp2(s - top)
         total = jnp.sum(p, axis=0, keepdims=True)
-        pt[h, lo:hi, :] = p.astype(BF16)
-        out = dot(kall[lo:hi, vcols(h)], pt[h, lo:hi, :], 0, 0)
+        pb = p.astype(BF16)
+        pt[h, rows, :] = pb
+        out = dot(kall[rows, vcols(h)], pb, 0, 0)
         return top, total, out
 
     lane_block = lax.div(iota((1, TOK), 1), 128)
-    rows_bias = []
-    for e in range(6):
-        vals = []
-        for i in range(2):
-            if e - i < 0 or e - i > 4:
-                vals.append(NEG_BIG)
-                continue
-            want = 2 * d - 2 + e
-            hit = jnp.int32(0)
-            for j in range(SLOTS):
-                ok = jnp.where(nb_ref[i, j] == want, 1, 0) * jnp.where(nc_ref[i] > j, 1, 0)
-                hit = jnp.maximum(hit, ok)
-            vals.append(jnp.where(hit > 0, 0.0, NEG_BIG))
-        row = jnp.where(lane_block == 0, vals[0], vals[1])
-        rows_bias.append(jnp.broadcast_to(row, (128, TOK)))
-    nbias = jnp.concatenate(rows_bias, axis=0)
+
+    def list_bias(first, count):
+        rows_bias = []
+        for e in range(count):
+            vals = []
+            for i in range(2):
+                hit = jnp.int32(0)
+                for j in range(SLOTS):
+                    ok = jnp.where(nb_ref[i, j] == first + e, 1, 0) * jnp.where(nc_ref[i] > j, 1, 0)
+                    hit = jnp.maximum(hit, ok)
+                vals.append(jnp.where(hit > 0, 0.0, NEG_BIG))
+            row = jnp.where(lane_block == 0, vals[0], vals[1])
+            rows_bias.append(jnp.broadcast_to(row, (128, TOK)))
+        return jnp.concatenate(rows_bias, axis=0)
+
+    near_p.wait_recv()
+    local_bias = list_bias(2 * d - 2 + 2 * across, 4)
+    inner = [group(h, local, local_bias) for h in range(2)]
+
+    p1 = pool_matrix(128, 1).astype(BF16)
+    part = kall[pl.ds(pl.multiple_of(across * 512, 256), TOK), :]
+    kall[NEAR : NEAR + 128, :] = dot(p1, part, 1, 0).astype(BF16)
+
     fwds = [None] * 4
 
     def relay(li):
@@ -205,40 +216,33 @@
 
     for li in range(4):
         relay(li)
-    near_p.wait_recv()
-
-    p1 = pool_matrix(128, 1).astype(BF16)
-    part = kall[pl.ds(pl.multiple_of((1 - core) * 512, 256), TOK), :]
-    kall[NEAR : NEAR + 128, :] = dot(p1, part, 1, 0).astype(BF16)
-
     for li in range(4):
         fwds[li].wait_recv()
     five = buf5[...].astype(F32)
     kall[ROWS - 128 : ROWS, 0:256] = five[:, 0:8, :].reshape(128, 256).astype(BF16)
     kall[ROWS - 128 : ROWS, 256:512] = five[:, 8:16, :].reshape(128, 256).astype(BF16)
 
-    coarse = [group(h, NEAR, ROWS, cbias[...]) for h in range(2)]
+    coarse = [group(h, far, cbias[...]) for h in range(2)]
+
     near_o.wait_recv()
-    near = [group(h, 0, NEAR, nbias) for h in range(2)]
+    beside_bias = list_bias(2 * d - 2 + 4 * core, 2)
+    outer = [group(h, beside, beside_bias) for h in range(2)]
 
     attn, alphas, scaled = [], [], []
     usum = jnp.zeros((1, TOK), F32)
     vsum = jnp.zeros((1, TOK), F32)
     for h in range(2):
-        m1, t1, o1 = near[h]
-        m2, t2, o2 = coarse[h]
-        top = jnp.maximum(m1, m2)
-        a1 = jnp.exp2(m1 - top)
-        a2 = jnp.exp2(m2 - top)
-        inv_total = 1.0 / (a1 * t1 + a2 * t2)
-        a1 = a1 * inv_total
-        a2 = a2 * inv_total
-        out = o1 * a1 + o2 * a2
+        parts = (coarse[h], inner[h], outer[h])
+        top = functools.reduce(jnp.maximum, [part[0] for part in parts])
+        factors = [jnp.exp2(part[0] - top) for part in parts]
+        inv_total = 1.0 / sum(f * part[1] for f, part in zip(factors, parts))
+        factors = [f * inv_total for f in factors]
+        out = sum(f * part[2] for f, part in zip(factors, parts))
         sc = out * hs_ref[h]
         usum = usum + jnp.sum(sc * sc, axis=0, keepdims=True)
         vsum = vsum + jnp.sum(sc * back[kcols(h), :], axis=0, keepdims=True)
         attn.append(out)
-        alphas.append((a1, a2))
+        alphas.append(factors)
         scaled.append(sc)
     ps_own[0:1, :] = usum
     ps_own[1:2, :] = vsum
@@ -270,18 +274,18 @@
         d_attn = (inv * hs_ref[h]) * (back[kcols(h), :] - scaled[h] * fac)
         d_group.append([(d_attn * a).astype(BF16) for a in alphas[h]])
 
-    def backward(h, g, lo, hi, keep, off):
+    def backward(h, g, rows, keep):
         dg = d_group[h][g]
         delta = jnp.sum(dg.astype(F32) * attn[h], axis=0, keepdims=True)
-        dp = dot(kall[lo:hi, vcols(h)], dg, 1, 0)
-        pg = pt[h, lo:hi, :]
+        dp = dot(kall[rows, vcols(h)], dg, 1, 0)
+        pg = pt[h, rows, :]
         ds = (pg.astype(F32) * (dp - delta)).astype(BF16)
-        dst[h, lo:hi, :] = ds
+        dst[h, rows, :] = ds
         keep[:, kcols(h)] = dot(ds, qv[:, kcols(h)], 1, 0) * SCALE
         keep[:, vcols(h)] = dot(pg, dg, 1, 1)
 
     for h in range(2):
-        backward(h, 1, NEAR, ROWS, cg, NEAR)
+        backward(h, 0, far, cg)
     for li in range(4):
         row = pl.multiple_of(128 * (li + 1) + core * 64, 64)
         c_send[64 * li : 64 * (li + 1), :] = cg[pl.ds(row, 64), :].astype(BF16)
@@ -289,16 +293,11 @@
     swap.start()
 
     for h in range(2):
-        backward(h, 0, 0, NEAR, ext, 0)
-    rim_out[1] = ext[pl.ds(pl.multiple_of(core * 512, 256), TOK), :].astype(BF16)
+        backward(h, 2, beside, ext_o)
+    rim_out[1] = ext_o[...].astype(BF16)
     rim_o = remote(rim_out.at[1], rim_in.at[1], rim_send.at[1], rim_recv.at[1], other, z)
     rim_o.start()
-    rim_out[0] = (
-        ext[pl.ds(pl.multiple_of((1 - core) * 512, 256), TOK), :]
-        + dot(e1, cg[0:128, :].astype(BF16), 1, 0)
-    ).astype(BF16)
-    rim_p = remote(rim_out.at[0], rim_in.at[0], rim_send.at[0], rim_recv.at[0], partner, z)
-    rim_p.start()
+    backward(0, 1, local, ext)
 
     swap.wait_recv()
     for li in (3, 2, 1, 0):
@@ -320,6 +319,14 @@
                 dst_ref = ret5.at[pos]
             remote(src, dst_ref, ret_send.at[li], ret_recv.at[li], (base + j) * 2 + across, z).start()
 
+    backward(1, 1, local, ext)
+    rim_out[0] = (
+        ext[pl.ds(pl.multiple_of(across * 256, 256), TOK), :]
+        + dot(e1, cg[0:128, :].astype(BF16), 1, 0)
+    ).astype(BF16)
+    rim_p = remote(rim_out.at[0], rim_in.at[0], rim_send.at[0], rim_recv.at[0], partner, z)
+    rim_p.start()
+
     for h in range(2):
         mixed_v[:, kcols(h)] = ((scaled[h] * inv).T * gain[:, kcols(h)]).astype(BF16)
     for h in range(2):
@@ -328,7 +335,7 @@
 
     rim_p.wait_recv()
     rim_o.wait_recv()
-    grad = ext[TOK : 2 * TOK, :] + rim_in[0].astype(F32) + rim_in[1].astype(F32)
+    grad = ext[pl.ds(pl.multiple_of(core * 256, 256), TOK), :] + rim_in[0].astype(F32) + rim_in[1].astype(F32)
     for li in range(3):
         wait_bytes(ret.at[pl.ds(64 * li, 64)], ret_recv.at[li])
     wait_bytes(ret5, ret_recv.at[3])
@@ -396,7 +403,7 @@
                 pltpu.VMEM((2, ROWS, TOK), BF16),
                 pltpu.VMEM((2, ROWS, TOK), BF16),
                 pltpu.VMEM((COARSE, COLS), F32),
-                pltpu.VMEM((NEAR, COLS), F32),
+                pltpu.VMEM((512, COLS), F32),
                 pltpu.VMEM((256, COLS), BF16),
                 pltpu.VMEM((256, COLS), BF16),
                 pltpu.VMEM((2, TOK, COLS), BF16),
@@ -405,6 +412,7 @@
                 pltpu.VMEM((8, 16, 256), BF16),
                 pltpu.VMEM((192, COLS), BF16),
                 pltpu.VMEM((8, 16, 256), BF16),
+                pltpu.VMEM((TOK, COLS), F32),
                 dma((8,)), dma((4,)), dma((4,)), dma((4,)), dma((4,)),
                 dma((2,)), dma((2,)), dma((2,)), dma((2,)), dma((2,)), dma((2,)),
                 dma((4,)), dma((4,)),

time: 45.3 us -> 44.3 us (0.978)
  Pallas kernels: 44.6 us -> 43.5 us
    pallas_call x1, Pallas kernels: 43.7 us -> 42.7 us  [body(): pl.pallas_call(functools.partial(kernel, n_ctx, n_head), out_shape=(pltpu...]
where the time goes in v5:
time: 44.3 us; the launch traced here: 44.2 us
  Pallas kernels  43.5 us (98%)
  between operations  0.64 us (1%)
    pallas_call x1, Pallas kernels, body(): pl.pallas_call(functools.partial(kernel, n_ctx, n_head), out_shape=(pltpu...  42.7 us

profile of v5, /device:TPU:1, one launch (start us, length us, event | category | flops | bytes accessed | tf_op | source)
XLA Modules:
  0.0 44.2 jit_solution(3009395508453247575)
XLA Ops:
  0.6 42.7 %shard_map.111 = (bf16[256,256]{1,0:T(8,128)(2,1)S(1)}, bf16[256,256]{1,0:T(8,128)(2,1)S(1)}, bf16[256,256]{1,0:T(8,128)(2,1)S(1)}, bf16[256,256]{1,0:T(8,128)(2,1)S(1)}) custom-call(bf16[256,256]{1,0:T(8,128)(2,1)} %q_hbm.1, bf16[256,256]{1,0:T(8,128)(2,1)} %k_hbm.1, bf16[256,256]{1,0:T(8,128)(2,1)} %v_hbm.1, s32[2,4]{1,0:T(2,128)} %nb_hbm.1, s32[2]{0:T(128)} %nc_hbm.1, ...), custom_call_target="tpu_custom_call" | custom-call | tf_op jit(solution)/shard_map/pallas_call | solution.py:383
  43.4 0.8 %shard_map.112 = (bf16[256,256]{1,0:T(8,128)(2,1)}, bf16[256,256]{1,0:T(8,128)(2,1)}, bf16[256,256]{1,0:T(8,128)(2,1)}, bf16[256,256]{1,0:T(8,128)(2,1)}) custom-call(bf16[256,256]{1,0:T(8,128)(2,1)S(1)} %get-tuple-element.8.a, bf16[256,256]{1,0:T(8,128)(2,1)S(1)} %get-tuple-element.9.b, bf16[256,256]{1,0:T(8,128)(2,1)S(1)} %get-tuple-element.10.c, ...), custom_call_target="tpu_custom_call" | custom-call | tf_op jit(solution)/shard_map/pallas_call | solution.py:424

commit v6 on v5

--- a/solution.py
+++ b/solution.py
@@ -246,7 +246,7 @@
         scaled.append(sc)
     ps_own[0:1, :] = usum
     ps_own[1:2, :] = vsum
-    for m in range(1, n_head):
+    for m in sorted(range(1, n_head), key=lambda m: -min(m, n_head - m)):
         remote(
             ps_own, ps_buf.at[m - 1], ps_sem.at[0], ps_sem.at[1], d, lax.rem(z + m, n_head)
         ).start()
@@ -274,33 +274,43 @@
         d_attn = (inv * hs_ref[h]) * (back[kcols(h), :] - scaled[h] * fac)
         d_group.append([(d_attn * a).astype(BF16) for a in alphas[h]])
 
-    def backward(h, g, rows, keep):
+    def backward(h, g, rows, keep, to=slice(None)):
         dg = d_group[h][g]
         delta = jnp.sum(dg.astype(F32) * attn[h], axis=0, keepdims=True)
         dp = dot(kall[rows, vcols(h)], dg, 1, 0)
         pg = pt[h, rows, :]
         ds = (pg.astype(F32) * (dp - delta)).astype(BF16)
         dst[h, rows, :] = ds
-        keep[:, kcols(h)] = dot(ds, qv[:, kcols(h)], 1, 0) * SCALE
-        keep[:, vcols(h)] = dot(pg, dg, 1, 1)
-
-    for h in range(2):
-        backward(h, 0, far, cg)
-    for li in range(4):
-        row = pl.multiple_of(128 * (li + 1) + core * 64, 64)
-        c_send[64 * li : 64 * (li + 1), :] = cg[pl.ds(row, 64), :].astype(BF16)
-    swap = remote(c_send, c_recv, cp_sem.at[0], cp_sem.at[1], partner, z)
-    swap.start()
+        keep[to, kcols(h)] = dot(ds, qv[:, kcols(h)], 1, 0) * SCALE
+        keep[to, vcols(h)] = dot(pg, dg, 1, 1)
 
     for h in range(2):
         backward(h, 2, beside, ext_o)
     rim_out[1] = ext_o[...].astype(BF16)
     rim_o = remote(rim_out.at[1], rim_in.at[1], rim_send.at[1], rim_recv.at[1], other, z)
     rim_o.start()
-    backward(0, 1, local, ext)
-
-    swap.wait_recv()
+    for h in range(2):
+        backward(h, 0, pl.ds(NEAR + 384, 256), cg, slice(384, 640))
+
+    def start_swap(lis, i):
+        for li in lis:
+            row = pl.multiple_of(128 * (li + 1) + core * 64, 64)
+            c_send[64 * li : 64 * (li + 1), :] = cg[pl.ds(row, 64), :].astype(BF16)
+        half = pl.ds(64 * lis[0], 128)
+        copy = remote(c_send.at[half], c_recv.at[half], cp_sem.at[i], cp_sem.at[2 + i], partner, z)
+        copy.start()
+        return copy
+
+    swap_far = start_swap((2, 3), 0)
+    for h in range(2):
+        backward(h, 0, pl.ds(NEAR, 384), cg, slice(0, 384))
+    swap = start_swap((0, 1), 1)
+
+    swap_far.wait_recv()
     for li in (3, 2, 1, 0):
+        if li == 1:
+            backward(0, 1, local, ext)
+            swap.wait_recv()
         row = pl.multiple_of(128 * (li + 1) + across * 64, 64)
         total = cg[pl.ds(row, 64), :] + c_recv[64 * li : 64 * (li + 1), :].astype(F32)
         if li < 3:
@@ -357,6 +367,7 @@
     near_o.wait_send()
     wait_bytes(ps_buf, ps_sem.at[0])
     swap.wait_send()
+    swap_far.wait_send()
     rim_p.wait_send()
     rim_o.wait_send()
 
@@ -414,7 +425,7 @@
                 pltpu.VMEM((8, 16, 256), BF16),
                 pltpu.VMEM((TOK, COLS), F32),
                 dma((8,)), dma((4,)), dma((4,)), dma((4,)), dma((4,)),
-                dma((2,)), dma((2,)), dma((2,)), dma((2,)), dma((2,)), dma((2,)),
+                dma((2,)), dma((2,)), dma((2,)), dma((4,)), dma((2,)), dma((2,)),
                 dma((4,)), dma((4,)),
             ],
             compiler_params=pltpu.CompilerParams(

time: 44.3 us -> 43.4 us (0.980)
  Pallas kernels: 43.5 us -> 42.6 us
    pallas_call x1, Pallas kernels: 42.7 us -> 41.8 us  [body(): pl.pallas_call(functools.partial(kernel, n_ctx, n_head), out_shape=(pltpu...]
where the time goes in v6:
time: 43.4 us; the launch traced here: 43.3 us
  Pallas kernels  42.6 us (98%)
  between operations  0.64 us (1%)
    pallas_call x1, Pallas kernels, body(): pl.pallas_call(functools.partial(kernel, n_ctx, n_head), out_shape=(pltpu...  41.8 us

profile of v6, /device:TPU:1, one launch (start us, length us, event | category | flops | bytes accessed | tf_op | source)
XLA Modules:
  0.0 43.3 jit_solution(12082403752624271474)
XLA Ops:
  0.6 41.8 %shard_map.111 = (bf16[256,256]{1,0:T(8,128)(2,1)S(1)}, bf16[256,256]{1,0:T(8,128)(2,1)S(1)}, bf16[256,256]{1,0:T(8,128)(2,1)S(1)}, bf16[256,256]{1,0:T(8,128)(2,1)S(1)}) custom-call(bf16[256,256]{1,0:T(8,128)(2,1)} %q_hbm.1, bf16[256,256]{1,0:T(8,128)(2,1)} %k_hbm.1, bf16[256,256]{1,0:T(8,128)(2,1)} %v_hbm.1, s32[2,4]{1,0:T(2,128)} %nb_hbm.1, s32[2]{0:T(128)} %nc_hbm.1, ...), custom_call_target="tpu_custom_call" | custom-call | tf_op jit(solution)/shard_map/pallas_call | solution.py:394
  42.4 0.8 %shard_map.112 = (bf16[256,256]{1,0:T(8,128)(2,1)}, bf16[256,256]{1,0:T(8,128)(2,1)}, bf16[256,256]{1,0:T(8,128)(2,1)}, bf16[256,256]{1,0:T(8,128)(2,1)}) custom-call(bf16[256,256]{1,0:T(8,128)(2,1)S(1)} %get-tuple-element.8.a, bf16[256,256]{1,0:T(8,128)(2,1)S(1)} %get-tuple-element.9.b, bf16[256,256]{1,0:T(8,128)(2,1)S(1)} %get-tuple-element.10.c, ...), custom_call_target="tpu_custom_call" | custom-call | tf_op jit(solution)/shard_map/pallas_call | solution.py:435

commit v7 on v6

--- a/solution.py
+++ b/solution.py
@@ -134,7 +134,6 @@
         near_send.at[1], near_recv.at[1], other, z,
     )
     near_p.start()
-    near_o.start()
 
     qb = lax.div(iota((128, TOK), 1), 128) + 2 * d
     r = iota((128, TOK), 0)
@@ -148,6 +147,7 @@
         cbias[128 * (li + 1) : 128 * (li + 2)] = jnp.where(
             jnp.abs((first >> 7) - qb) > 2, float(li + 2), NEG_BIG
         )
+    near_o.start()
     loads[3].wait()
     loads[4].wait()
     gain = gain_v[...].reshape(1, 256)

time: 43.4 us -> 43.4 us (level)
  no operation moved by 1% of the time
where the time goes in v7:
time: 43.4 us; the launch traced here: 43.3 us
  Pallas kernels  42.6 us (98%)
  between operations  0.64 us (1%)
    pallas_call x1, Pallas kernels, body(): pl.pallas_call(functools.partial(kernel, n_ctx, n_head), out_shape=(pltpu...  41.8 us

profile of v7, /device:TPU:1, one launch (start us, length us, event | category | flops | bytes accessed | tf_op | source)
XLA Modules:
  0.0 43.3 jit_solution(12082403752624271474)
XLA Ops:
  0.6 41.8 %shard_map.111 = (bf16[256,256]{1,0:T(8,128)(2,1)S(1)}, bf16[256,256]{1,0:T(8,128)(2,1)S(1)}, bf16[256,256]{1,0:T(8,128)(2,1)S(1)}, bf16[256,256]{1,0:T(8,128)(2,1)S(1)}) custom-call(bf16[256,256]{1,0:T(8,128)(2,1)} %q_hbm.1, bf16[256,256]{1,0:T(8,128)(2,1)} %k_hbm.1, bf16[256,256]{1,0:T(8,128)(2,1)} %v_hbm.1, s32[2,4]{1,0:T(2,128)} %nb_hbm.1, s32[2]{0:T(128)} %nc_hbm.1, ...), custom_call_target="tpu_custom_call" | custom-call | tf_op jit(solution)/shard_map/pallas_call | solution.py:394
  42.4 0.8 %shard_map.112 = (bf16[256,256]{1,0:T(8,128)(2,1)}, bf16[256,256]{1,0:T(8,128)(2,1)}, bf16[256,256]{1,0:T(8,128)(2,1)}, bf16[256,256]{1,0:T(8,128)(2,1)}) custom-call(bf16[256,256]{1,0:T(8,128)(2,1)S(1)} %get-tuple-element.8.a, bf16[256,256]{1,0:T(8,128)(2,1)S(1)} %get-tuple-element.9.b, bf16[256,256]{1,0:T(8,128)(2,1)S(1)} %get-tuple-element.10.c, ...), custom_call_target="tpu_custom_call" | custom-call | tf_op jit(solution)/shard_map/pallas_call | solution.py:435
